TPU v7x, 256 devices: a whole 4x4x8 slice. The times are simulated.
256 devices in a mesh: gy: 8 (over z_hi, core), gz: 32 (over y, x, z_lo).
Axes of the slice: x: 4, y: 4, z: 8 (z_hi: 4, z_lo: 2; z = z_hi * 2 + z_lo), core: 2. Of those that a mesh axis runs over, the one named last changes fastest.
Arguments:
- ex: float32 [128, 256, 512], P('gy', 'gz'), may hold values from -6 to 6
- ey: float32 [128, 256, 512], P('gy', 'gz'), may hold values from -6 to 6
- ez: float32 [128, 256, 512], P('gy', 'gz'), may hold values from -6 to 6
- hx: float32 [128, 256, 512], P('gy', 'gz'), may hold values from -6 to 6
- hy: float32 [128, 256, 512], P('gy', 'gz'), may hold values from -6 to 6
- hz: float32 [128, 256, 512], P('gy', 'gz'), may hold values from -6 to 6
- material: int32 [128, 256, 512], P('gy', 'gz'), may hold values from 0 to 15
- eps_table: float32 [16], replicated, may hold values from 1 to 4
- mu_table: float32 [16], replicated, may hold values from 1 to 2
Outputs:
- ex_new: float32 [128, 256, 512], P('gy', 'gz')
- ey_new: float32 [128, 256, 512], P('gy', 'gz')
- ez_new: float32 [128, 256, 512], P('gy', 'gz')
- hx_new: float32 [128, 256, 512], P('gy', 'gz')
- hy_new: float32 [128, 256, 512], P('gy', 'gz')
- hz_new: float32 [128, 256, 512], P('gy', 'gz')
Inputs may be any that keep to these rules, and one draw needn't show every extreme that they name: material indexes the two tables.
All inputs are finite; a program needn't handle non-finite values.
Results may differ from a plain program's by a relative error of at most 0.00026.
Values sent between devices are 32-bit elements; how exact they have to be, the bound alone decides.
No kernel may reach another device: no remote copies, remote signals or barrier semaphores. Data moves between devices by JAX's collectives and lax.ppermute only.
A program may use at most 128 MiB of HBM per device.

v0:
```python
import functools

import jax
import jax.numpy as jnp
from jax import lax
from jax.experimental import pallas as pl
from jax.experimental.pallas import tpu as pltpu
from jax.sharding import PartitionSpec as P

courant = 16.0
F32 = jnp.float32
NYL, NZL, NX = 16, 8, 512
ROWS = NYL * NZL
LANES = 128
CHUNKS = NX // LANES
RUN = NX // 8

Y_STEPS = ((1, 0), (2, 1), (6, 2))
Z_STEPS = ((1, 0), (2, 1), (6, 2), (8, 3), (24, 4))


def shifted(array, axis, by):
    size = lax.axis_size(axis)
    pairs = [(i, i + by) for i in range(size) if 0 <= i + by < size]
    return lax.ppermute(array, axis, pairs)


def swapped(array, axis, flip):
    size = lax.axis_size(axis)
    return lax.ppermute(array, axis, [(i, i ^ flip) for i in range(size)])


def merge_mat(s1, s2):
    ga1, b1, gc1 = s1
    ga2, b2, gc2 = s2
    ground = ga2 if gc1 is None else gc1 + ga2
    inv = 1.0 / (b1 + b2 + ground)
    p, q = b1 * inv, b2 * inv
    right = q * ground
    return (ga1 + p * ground, p * b2, right if gc2 is None else gc2 + right), (p, q, inv)


def merge_rhs(r1, r2, p, q):
    w = r1[1] + r2[0]
    return (r1[0] + p * w, r2[1] + q * w), w


def tree_mat(lo, hi, leaf, put):
    if hi - lo == 1:
        return leaf(lo)
    mid = (lo + hi) // 2
    left = tree_mat(lo, mid, leaf, put)
    right = tree_mat(mid, hi, leaf, put)
    stamp, coefs = merge_mat(left, right)
    put(mid - 1, coefs)
    return stamp


def tree_rhs(lo, hi, leaf, coef, put):
    if hi - lo == 1:
        return leaf(lo)
    mid = (lo + hi) // 2
    left = tree_rhs(lo, mid, leaf, coef, put)
    right = tree_rhs(mid, hi, leaf, coef, put)
    out, w = merge_rhs(left, right, coef(0, mid - 1), coef(1, mid - 1))
    put(mid - 1, w)
    return out


def tree_down(lo, hi, x_lo, x_hi, coef, source, put):
    if hi - lo == 1:
        put(lo, x_lo, x_hi)
        return
    mid = (lo + hi) // 2
    k = mid - 1
    x_mid = coef(0, k) * x_lo + coef(1, k) * x_hi + coef(2, k) * source(k)
    tree_down(lo, mid, x_lo, x_mid, coef, source, put)
    tree_down(mid, hi, x_mid, x_hi, coef, source, put)


def cut(c):
    return pl.ds(c * LANES, LANES)


def plain(y):
    return pl.ds(y * NZL, NZL)


def yrow(y, c):
    return pl.ds((y * CHUNKS + c) * NZL, NZL)


def zrow(z, c):
    return pl.ds(c * NZL + z, NYL, stride=CHUNKS * NZL)


def wide(ref, y):
    return jnp.concatenate([ref[yrow(y, c), :] for c in range(CHUNKS)], axis=1)


def put_wide(ref, y, value):
    for c in range(CHUNKS):
        ref[yrow(y, c), :] = value[:, c * LANES:(c + 1) * LANES]


def tall(ref, c):
    return jnp.concatenate([ref[yrow(y, c), :] for y in range(NYL)], axis=0)


def next_x(v):
    lane = lax.broadcasted_iota(jnp.int32, v.shape, 1)
    return jnp.where(lane == NX - 1, 0.0, pltpu.roll(v, NX - 1, 1))


def prev_x(v):
    lane = lax.broadcasted_iota(jnp.int32, v.shape, 1)
    return jnp.where(lane == 0, 0.0, pltpu.roll(v, 1, 1))


def bit_of(axis, bit):
    return (lax.axis_index(axis) >> bit) & 1


def rims_kernel(hy, ez, ex, hx, hy_top, ez_first, ex_first, hx_last):
    ez_first[...] = ez[...]
    hx_last[...] = hx[...]
    for y in range(NYL):
        hy_top[y:y + 1, :] = hy[(y + 1) * NZL - 1:(y + 1) * NZL, :]
        ex_first[y:y + 1, :] = ex[y * NZL:y * NZL + 1, :]


def bands_kernel(material, eps, mu, ie, ch, y_mat, z_mat, cy, cz):
    for y in range(NYL):
        for c in range(CHUNKS):
            label = material[plain(y), cut(c)]
            e_val = jnp.full(label.shape, eps[0], F32)
            m_val = jnp.full(label.shape, mu[0], F32)
            for k in range(1, 16):
                hit = label == k
                e_val = jnp.where(hit, eps[k], e_val)
                m_val = jnp.where(hit, mu[k], m_val)
            ie[yrow(y, c), :] = e_val * (1.0 / courant)
            ch[yrow(y, c), :] = courant / m_val
    for c in range(CHUNKS):
        for rows, count, mat, coef in ((yrow, NYL, y_mat, cy), (zrow, NZL, z_mat, cz)):

            def leaf(i):
                return ie[rows(i, c), :], ch[rows(i, c), :], None

            def put(k, coefs):
                for j in range(3):
                    coef[j * (count - 1) + k, :, cut(c)] = coefs[j]

            for j, part in enumerate(tree_mat(0, count, leaf, put)):
                mat[j, :, cut(c)] = part


def up_local(rows, count, c, f_of, g_of, coef, w_out, pay):
    def leaf(i):
        return f_of[rows(i, c), :], g_of[rows(i, c), :]

    def get(j, k):
        return coef[j * (count - 1) + k, :, cut(c)]

    def put(k, w):
        w_out[k, :, cut(c)] = w

    f, g = tree_rhs(0, count, leaf, get, put)
    pay[0, :, cut(c)] = f
    pay[1, :, cut(c)] = g


def first_y_kernel(hz, ey, ex, hy, hy_rim, ie, ch, y_mat, cy, pay, w_out, hz_t, f_s, g_s):
    for y in range(NYL):
        r = plain(y)
        ey_r = ey[r, :]
        ht = hz[r, :] - wide(ch, y) * (next_x(ey_r) - ey_r)
        hy_r = hy[r, :]
        z_of = lax.broadcasted_iota(jnp.int32, hy_r.shape, 0)
        low = jnp.where(z_of == 0, jnp.broadcast_to(hy_rim[y:y + 1, :], hy_r.shape), pltpu.roll(hy_r, 1, 0))
        put_wide(hz_t, y, ht)
        put_wide(f_s, y, wide(ie, y) * ex[r, :] - (hy_r - low) + ht)
        put_wide(g_s, y, -ht)
    for c in range(CHUNKS):
        up_local(yrow, NYL, c, f_s, g_s, cy, w_out, pay)
    pay[2:5] = y_mat[...]


def first_z_kernel(hx, ez, ez_rim, hz, ey, ie, ch, z_mat, cz, pay, w_out, hx_t, f_s, g_s):
    for y in range(NYL):
        r = plain(y)
        up = ez[plain(y + 1), :] if y < NYL - 1 else ez_rim[...]
        ht = hx[r, :] - wide(ch, y) * (up - ez[r, :])
        hz_r = hz[r, :]
        put_wide(hx_t, y, ht)
        put_wide(f_s, y, wide(ie, y) * ey[r, :] - (hz_r - prev_x(hz_r)) + ht)
        put_wide(g_s, y, -ht)
    for c in range(CHUNKS):
        up_local(zrow, NZL, c, f_s, g_s, cz, w_out, pay)
    pay[2:5] = z_mat[...]


def merge_all(lower, upper, pay, save):
    stamp, (p, q, inv) = merge_mat((lower[2], lower[3], lower[4]), (upper[2], upper[3], upper[4]))
    (f, g), w = merge_rhs((lower[0], lower[1]), (upper[0], upper[1]), p, q)
    pay[0], pay[1], pay[2], pay[3], pay[4] = f, g, *stamp
    save[0], save[1], save[2], save[3] = p, q, inv, w


def merge_kernel(axis, bit, mine, other, pay, save):
    side = bit_of(axis, bit)

    @pl.when(side == 0)
    def _():
        merge_all(mine, other, pay, save)

    @pl.when(side == 1)
    def _():
        merge_all(other, mine, pay, save)


def again_all(lower, upper, kept, pay, w_out):
    (f, g), w = merge_rhs((lower[0], lower[1]), (upper[0], upper[1]), kept[0], kept[1])
    pay[0], pay[1] = f, g
    w_out[...] = w


def again_kernel(axis, bit, mine, other, kept, pay, w_out):
    side = bit_of(axis, bit)

    @pl.when(side == 0)
    def _():
        again_all(mine, other, kept, pay, w_out)

    @pl.when(side == 1)
    def _():
        again_all(other, mine, kept, pay, w_out)


def ends_of(axis, levels, sources, f, total):
    x_lo = f / total
    x_hi = jnp.zeros_like(x_lo)
    for bit in reversed(range(len(levels))):
        kept = levels[bit]
        x_mid = kept[0] * x_lo + kept[1] * x_hi + kept[2] * sources[bit]
        upper = jnp.broadcast_to(bit_of(axis, bit), x_lo.shape) == 1
        x_lo, x_hi = jnp.where(upper, x_mid, x_lo), jnp.where(upper, x_hi, x_mid)
    return x_lo, x_hi


def down_local(rows, count, c, x_lo, x_hi, coef, w_of, put):
    def get(j, k):
        return coef[j * (count - 1) + k, :, cut(c)]

    def source(k):
        return w_of[k, :, cut(c)]

    tree_down(0, count, x_lo[:, cut(c)], x_hi[:, cut(c)], get, source, put)


def mid_y_kernel(pay3, s0, s1, s2, cy, w_y, hz_t, hy, hy_u, ex, ie, ch, cz,
                 hz_u, pay, w_out, lo_s, hi_s, f_s, g_s):
    levels = (s0, s1, s2)
    lo_s[...], hi_s[...] = ends_of("gy", levels, [s[3] for s in levels], pay3[0], pay3[2] + pay3[3])
    for c in range(CHUNKS):

        def put(y, x, x_next):
            r = yrow(y, c)
            hz_u[r, :] = hz_t[r, :] + 2.0 * (ch[r, :] * (x_next - x))
            s = hy[plain(y), cut(c)] - hy_u[r, :]
            f_s[r, :] = ie[r, :] * (2.0 * x - ex[plain(y), cut(c)]) + s
            g_s[r, :] = -s

        down_local(yrow, NYL, c, lo_s, hi_s, cy, w_y, put)
        up_local(zrow, NZL, c, f_s, g_s, cz, w_out, pay)


def mid_z_kernel(pay5, s0, s1, s2, s3, s4, cz, w_z, hx_t, hx, ez1, ez, ie, ch, cy,
                 ey1, hx_u, pay, w_out, lo_s, hi_s, f_s, g_s):
    levels = (s0, s1, s2, s3, s4)
    lo_s[...], hi_s[...] = ends_of("gz", levels, [s[3] for s in levels], pay5[0], pay5[2] + pay5[3])
    for c in range(CHUNKS):

        def put(z, x, x_next):
            r = zrow(z, c)
            ey1[r, :] = x
            hx_u[r, :] = hx_t[r, :] + 2.0 * (ch[r, :] * (x_next - x))

        down_local(zrow, NZL, c, lo_s, hi_s, cz, w_z, put)
        for y in range(NYL):
            r = yrow(y, c)
            n = plain(y)
            s = hx[n, cut(c)] - hx_u[r, :]
            f_s[r, :] = ie[r, :] * (2.0 * ez1[n, cut(c)] - ez[n, cut(c)]) + s
            g_s[r, :] = -s
        up_local(yrow, NYL, c, f_s, g_s, cy, w_out, pay)


def end_kernel(axis, rows, count, steps, *refs):
    pay, total = refs[0], refs[1]
    levels, sources = refs[2:2 + steps], refs[2 + steps:2 + 2 * steps]
    coef, w_of, h_u, ch, e_new, h_new, lo_s, hi_s, e_s, h_s = refs[2 + 2 * steps:]
    lo_s[...], hi_s[...] = ends_of(axis, levels, [s[...] for s in sources], pay[0], total[2] + total[3])
    for c in range(CHUNKS):

        def put(i, x, x_next):
            r = rows(i, c)
            e_s[r, :] = x
            h_s[r, :] = h_u[r, :] - ch[r, :] * (x_next - x)

        down_local(rows, count, c, lo_s, hi_s, coef, w_of, put)
        for y in range(NYL):
            e_new[plain(y), cut(c)] = e_s[yrow(y, c), :]
            h_new[plain(y), cut(c)] = h_s[yrow(y, c), :]


def run_row(t):
    return pl.ds(t, 8, stride=RUN)


def x_solve(rhs, ie, ch, cx, keep, x_out, r_t, e_t, h_t, w_s):
    for c in range(CHUNKS):
        r_t[cut(c), :] = rhs[:, cut(c)].T
        if keep:
            e_t[cut(c), :] = tall(ie, c).T
            h_t[cut(c), :] = tall(ch, c).T
    inner = RUN - 1
    merges = inner + 3

    def put_coefs(k, coefs):
        for j in range(3):
            cx[j * merges + k] = coefs[j]

    def get(j, k):
        return cx[j * merges + k]

    def source(k):
        return w_s[k]

    def put_w(k, w):
        w_s[k] = w

    spot = lax.broadcasted_iota(jnp.int32, (8, LANES), 0)
    if keep:
        stamp = tree_mat(0, RUN, lambda t: (e_t[run_row(t), :], h_t[run_row(t), :], None), put_coefs)
        for step in range(3):
            nearby = tuple(pltpu.roll(part, 8 - (1 << step), 0) for part in stamp)
            stamp, coefs = merge_mat(stamp, nearby)
            put_coefs(inner + step, coefs)
        cx[3 * merges] = stamp[0] + stamp[1]
    pair = tree_rhs(0, RUN, lambda t: (r_t[run_row(t), :], jnp.zeros((8, LANES), F32)), get, put_w)
    for step in range(3):
        nearby = tuple(pltpu.roll(part, 8 - (1 << step), 0) for part in pair)
        pair, w = merge_rhs(pair, nearby, get(0, inner + step), get(1, inner + step))
        put_w(inner + step, w)
    x_lo = pair[0] / cx[3 * merges]
    x_hi = jnp.zeros_like(x_lo)
    for step in reversed(range(3)):
        k = inner + step
        x_mid = get(0, k) * x_lo + get(1, k) * x_hi + get(2, k) * source(k)
        upper = ((spot >> step) & 1) == 1
        x_lo, x_hi = (jnp.where(upper, pltpu.roll(x_mid, 1 << step, 0), x_lo),
                      jnp.where(upper, pltpu.roll(x_hi, 1 << step, 0), x_mid))

    def put_x(t, x, x_next):
        r_t[run_row(t), :] = x

    tree_down(0, RUN, x_lo, x_hi, get, source, put_x)
    for c in range(CHUNKS):
        x_out[:, cut(c)] = r_t[cut(c), :].T


def first_x_kernel(hy, ex, ex_rim, hx, hx_rim, ez, ie, ch, ez1, hy_u, cx, r_t, e_t, h_t, w_s, rhs):
    for y in range(NYL):
        r = plain(y)
        ex_r = ex[r, :]
        z_of = lax.broadcasted_iota(jnp.int32, ex_r.shape, 0)
        up = jnp.where(z_of == NZL - 1, jnp.broadcast_to(ex_rim[y:y + 1, :], ex_r.shape), pltpu.roll(ex_r, NZL - 1, 0))
        ht = hy[r, :] - wide(ch, y) * (up - ex_r)
        low = hx[plain(y - 1), :] if y > 0 else hx_rim[...]
        put_wide(hy_u, y, ht)
        rhs[r, :] = wide(ie, y) * ez[r, :] + (ht - prev_x(ht)) - (hx[r, :] - low)
    x_solve(rhs, ie, ch, cx, True, ez1, r_t, e_t, h_t, w_s)
    for y in range(NYL):
        x = ez1[plain(y), :]
        put_wide(hy_u, y, wide(hy_u, y) + 2.0 * (wide(ch, y) * (next_x(x) - x)))


def last_x_kernel(ey1, ey, hz, hz_u, ie, ch, cx, ey_new, hz_new, r_t, w_s, rhs):
    for y in range(NYL):
        r = plain(y)
        s = hz[r, :] - wide(hz_u, y)
        rhs[r, :] = wide(ie, y) * (2.0 * wide(ey1, y) - ey[r, :]) + (s - prev_x(s))
    x_solve(rhs, ie, ch, cx, False, ey_new, r_t, None, None, w_s)
    for y in range(NYL):
        r = plain(y)
        x = ey_new[r, :]
        hz_new[r, :] = wide(hz_u, y) - wide(ch, y) * (next_x(x) - x)


VM = pl.BlockSpec(memory_space=pltpu.VMEM)
SM = pl.BlockSpec(memory_space=pltpu.SMEM)


def shape(*dims):
    return jax.ShapeDtypeStruct(dims, F32)


def call(kernel, args, outs, scratch=(), specs=None, name=None, flops=100000):
    return pl.pallas_call(
        kernel,
        out_shape=[shape(*dims) for dims in outs],
        in_specs=specs or [VM] * len(args),
        out_specs=[VM] * len(outs),
        scratch_shapes=[pltpu.VMEM(dims, F32) for dims in scratch],
        compiler_params=pltpu.CompilerParams(vmem_limit_bytes=40 * 1024 * 1024),
        name=name,
    )(*args)


FIELD = (ROWS, NX)
PACKED = (ROWS * CHUNKS, LANES)
Y1, Z1 = (NZL, NX), (NYL, NX)


def on_device(ex, ey, ez, hx, hy, hz, material, eps_table, mu_table):
    ex, ey, ez, hx, hy, hz, material = (a.reshape(FIELD) for a in (ex, ey, ez, hx, hy, hz, material))

    whole = pl.BlockSpec(FIELD, lambda i: (0, 0))
    hy_top, ez_first, ex_first, hx_last = pl.pallas_call(
        rims_kernel,
        grid=(1,),
        out_shape=[shape(*Z1), shape(*Y1), shape(*Z1), shape(*Y1)],
        in_specs=[whole, pl.BlockSpec(Y1, lambda i: (0, 0)), whole, pl.BlockSpec(Y1, lambda i: (NYL - 1, 0))],
        out_specs=[pl.BlockSpec(Z1, lambda i: (0, 0)), pl.BlockSpec(Y1, lambda i: (0, 0)),
                   pl.BlockSpec(Z1, lambda i: (0, 0)), pl.BlockSpec(Y1, lambda i: (0, 0))],
        name="rims",
    )(hy, ez, ex, hx)
    hy_rim = shifted(hy_top, "gz", 1)
    ez_rim = shifted(ez_first, "gy", -1)
    ex_rim = shifted(ex_first, "gz", -1)
    hx_rim = shifted(hx_last, "gy", 1)

    ie, ch, y_mat, z_mat, cy, cz = call(
        bands_kernel, (material, eps_table, mu_table),
        (PACKED, PACKED, (3,) + Y1, (3,) + Z1, (45,) + Y1, (21,) + Z1), specs=[VM, SM, SM], name="bands")

    pay_y, w_y, hz_t = call(first_y_kernel, (hz, ey, ex, hy, hy_rim, ie, ch, y_mat, cy),
                            ((5,) + Y1, (15,) + Y1, PACKED), (PACKED, PACKED), name="first_y")
    pay_z, w_z, hx_t = call(first_z_kernel, (hx, ez, ez_rim, hz, ey, ie, ch, z_mat, cz),
                            ((5,) + Z1, (7,) + Z1, PACKED), (PACKED, PACKED), name="first_z")

    def merge(pay, axis, step, plane):
        flip, bit = step
        other = swapped(pay, axis, flip)
        return call(functools.partial(merge_kernel, axis, bit), (pay, other), ((5,) + plane, (4,) + plane), name="merge")

    def again(pay, axis, step, plane, kept):
        flip, bit = step
        other = swapped(pay, axis, flip)
        return call(functools.partial(again_kernel, axis, bit), (pay, other, kept), ((2,) + plane, plane), name="again")

    ez1, hy_u, cx = call(first_x_kernel, (hy, ex, ex_rim, hx, hx_rim, ez, ie, ch),
                         (FIELD, PACKED, (3 * (RUN + 2) + 1, 8, LANES)),
                         ((NX, LANES), (NX, LANES), (NX, LANES), (RUN + 2, 8, LANES), FIELD), name="first_x")

    save_y = []
    for step in Y_STEPS:
        pay_y, kept = merge(pay_y, "gy", step, Y1)
        save_y.append(kept)
    hz_u, pay_z2, w_z2 = call(
        mid_y_kernel, (pay_y, *save_y, cy, w_y, hz_t, hy, hy_u, ex, ie, ch, cz),
        (PACKED, (2,) + Z1, (7,) + Z1), (Y1, Y1, PACKED, PACKED), name="mid_y")

    save_z = []
    for step in Z_STEPS:
        pay_z, kept = merge(pay_z, "gz", step, Z1)
        save_z.append(kept)
    ey1, hx_u, pay_y2, w_y2 = call(
        mid_z_kernel, (pay_z, *save_z, cz, w_z, hx_t, hx, ez1, ez, ie, ch, cy),
        (PACKED, PACKED, (2,) + Y1, (15,) + Y1), (Z1, Z1, PACKED, PACKED), name="mid_z")

    from_z = []
    for step, kept in zip(Z_STEPS, save_z):
        pay_z2, w = again(pay_z2, "gz", step, Z1, kept)
        from_z.append(w)
    ex_new, hy_new = call(
        functools.partial(end_kernel, "gz", zrow, NZL, 5), (pay_z2, pay_z, *save_z, *from_z, cz, w_z2, hy_u, ch),
        (FIELD, FIELD), (Z1, Z1, PACKED, PACKED), name="end_z")

    from_y = []
    for step, kept in zip(Y_STEPS, save_y):
        pay_y2, w = again(pay_y2, "gy", step, Y1, kept)
        from_y.append(w)
    ez_new, hx_new = call(
        functools.partial(end_kernel, "gy", yrow, NYL, 3), (pay_y2, pay_y, *save_y, *from_y, cy, w_y2, hx_u, ch),
        (FIELD, FIELD), (Y1, Y1, PACKED, PACKED), name="end_y")

    ey_new, hz_new = call(last_x_kernel, (ey1, ey, hz, hz_u, ie, ch, cx), (FIELD, FIELD),
                          ((NX, LANES), (RUN + 2, 8, LANES), FIELD), name="last_x")

    return tuple(a.reshape(NYL, NZL, NX) for a in (ex_new, ey_new, ez_new, hx_new, hy_new, hz_new))


def solution(mesh):
    cells = P("gy", "gz", None)
    return jax.shard_map(
        on_device,
        mesh=mesh,
        in_specs=(cells,) * 7 + (P(), P()),
        out_specs=(cells,) * 6,
        check_vma=False,
    )
```

profile of v0, /device:TPU:32, one launch (start us, length us, event | category | flops | bytes accessed | tf_op | source)
XLA Modules:
  0.0 80.5 jit_solution(17354312508845698609)
XLA Ops:
  0.7 1.8 %rims.1 = (f32[16,512]{1,0:T(8,128)}, f32[8,512]{1,0:T(8,128)}, f32[16,512]{1,0:T(8,128)}, f32[8,512]{1,0:T(8,128)}) custom-call(f32[128,512]{1,0:T(8,128)} %bitcast.17, f32[128,512]{1,0:T(8,128)} %bitcast.21, f32[128,512]{1,0:T(8,128)} %bitcast.13, f32[128,512]{1,0:T(8,128)} %bitcast.25), custom_call_target="tpu_custom_call" | custom-call | tf_op jit(solution)/shard_map/rims/pallas_call | solution.py:430
  6.6 1.9 %collective-permute-start.8 = (f32[5,16,512]{2,1,0:T(8,128)S(1)}, f32[5,16,512]{2,1,0:T(8,128)S(1)}, u32[]{:S(2)}, u32[]{:S(2)}) collective-permute-start(f32[5,16,512]{2,1,0:T(8,128)S(1)} %get-tuple-element.91.mine), channel_id=1, source_target_pairs={{0,1},{1,0},{2,3},{3,2},{4,5},{5,4},{6,7},{7,6},{8,9},{9,8},{10,11... | collective-permute-start | bytes 491528 | tf_op jit(solution)/shard_map/ppermute | solution.py:30
  8.5 3.5 %collective-permute-done.8.other = f32[5,16,512]{2,1,0:T(8,128)S(1)} collective-permute-done((f32[5,16,512]{2,1,0:T(8,128)S(1)}, f32[5,16,512]{2,1,0:T(8,128)S(1)}, u32[]{:S(2)}, u32[]{:S(2)}) %collective-permute-start.8) | collective-permute-done | bytes 163872 | tf_op jit(solution)/shard_map/ppermute | solution.py:30
  12.0 1.6 %collective-permute-start.10 = (f32[5,16,512]{2,1,0:T(8,128)S(1)}, f32[5,16,512]{2,1,0:T(8,128)S(1)}, u32[]{:S(2)}, u32[]{:S(2)}) collective-permute-start(f32[5,16,512]{2,1,0:T(8,128)S(1)} %get-tuple-element.94.mine), channel_id=1, source_target_pairs={{0,2},{1,3},{2,0},{3,1},{4,6},{5,7},{6,4},{7,5},{8,10},{9,11},{10,... | collective-permute-start | bytes 491528 | tf_op jit(solution)/shard_map/ppermute | solution.py:30
  13.6 4.4 %collective-permute-start = (f32[16,512]{1,0:T(8,128)S(1)}, f32[16,512]{1,0:T(8,128)S(1)}, u32[]{:S(2)}, u32[]{:S(2)}) collective-permute-start(f32[16,512]{1,0:T(8,128)S(1)} %copy-done.10), channel_id=1, source_target_pairs={{0,1},{1,2},{2,3},{3,4},{4,5},{5,6},{6,7},{7,8},{8,9},{9,10},{10,1... | collective-permute-start | bytes 98312 | tf_op jit(solution)/shard_map/ppermute | solution.py:25
  18.0 2.5 %collective-permute-start.12 = (f32[5,16,512]{2,1,0:T(8,128)S(1)}, f32[5,16,512]{2,1,0:T(8,128)S(1)}, u32[]{:S(2)}, u32[]{:S(2)}) collective-permute-start(f32[5,16,512]{2,1,0:T(8,128)S(1)} %get-tuple-element.97.mine), channel_id=1, source_target_pairs={{0,6},{1,7},{2,4},{3,5},{4,2},{5,3},{6,0},{7,1},{8,14},{9,15},{10,... | collective-permute-start | bytes 491528 | tf_op jit(solution)/shard_map/ppermute | solution.py:30
  22.8 4.2 %collective-permute-start.2 = (f32[5,8,512]{2,1,0:T(8,128)S(1)}, f32[5,8,512]{2,1,0:T(8,128)S(1)}, u32[]{:S(2)}, u32[]{:S(2)}) collective-permute-start(f32[5,8,512]{2,1,0:T(8,128)S(1)} %get-tuple-element.76.mine), channel_id=1, source_target_pairs={{0,64},{32,96},{64,0},{96,32},{128,192},{160,224},{192,128},{224,1... | collective-permute-start | bytes 245768 | tf_op jit(solution)/shard_map/ppermute | solution.py:30
  27.1 1.7 %collective-permute-start.14 = (f32[5,16,512]{2,1,0:T(8,128)S(1)}, f32[5,16,512]{2,1,0:T(8,128)S(1)}, u32[]{:S(2)}, u32[]{:S(2)}) collective-permute-start(f32[5,16,512]{2,1,0:T(8,128)S(1)} %get-tuple-element.100.mine), channel_id=1, source_target_pairs={{0,8},{1,9},{2,10},{3,11},{4,12},{5,13},{6,14},{7,15},{8,0},{9,1},... | collective-permute-start | bytes 491528 | tf_op jit(solution)/shard_map/ppermute | solution.py:30
  28.7 2.2 %collective-permute-done.2.other = f32[5,8,512]{2,1,0:T(8,128)S(1)} collective-permute-done((f32[5,8,512]{2,1,0:T(8,128)S(1)}, f32[5,8,512]{2,1,0:T(8,128)S(1)}, u32[]{:S(2)}, u32[]{:S(2)}) %collective-permute-start.2) | collective-permute-done | bytes 81952 | tf_op jit(solution)/shard_map/ppermute | solution.py:30
  31.0 5.1 %collective-permute-start.3 = (f32[5,8,512]{2,1,0:T(8,128)S(1)}, f32[5,8,512]{2,1,0:T(8,128)S(1)}, u32[]{:S(2)}, u32[]{:S(2)}) collective-permute-start(f32[5,8,512]{2,1,0:T(8,128)S(1)} %get-tuple-element.77.mine), channel_id=1, source_target_pairs={{0,192},{32,224},{64,128},{96,160},{128,64},{160,96},{192,0},{224,... | collective-permute-start | bytes 245768 | tf_op jit(solution)/shard_map/ppermute | solution.py:30
  36.1 1.9 %collective-permute-start.4 = (f32[16,512]{1,0:T(8,128)S(1)}, f32[16,512]{1,0:T(8,128)S(1)}, u32[]{:S(2)}, u32[]{:S(2)}) collective-permute-start(f32[16,512]{1,0:T(8,128)S(1)} %copy-done.9), channel_id=1, source_target_pairs={{1,0},{2,1},{3,2},{4,3},{5,4},{6,5},{7,6},{8,7},{9,8},{10,9},{11,1... | collective-permute-start | bytes 98312 | tf_op jit(solution)/shard_map/ppermute | solution.py:25
  40.1 2.6 %collective-permute-done.4.ex_rim = f32[16,512]{1,0:T(8,128)S(1)} collective-permute-done((f32[16,512]{1,0:T(8,128)S(1)}, f32[16,512]{1,0:T(8,128)S(1)}, u32[]{:S(2)}, u32[]{:S(2)}) %collective-permute-start.4) | collective-permute-done | bytes 32800 | tf_op jit(solution)/shard_map/ppermute | solution.py:25
  42.8 1.4 %first_x.1 = (f32[128,512]{1,0:T(8,128)S(1)}, f32[512,128]{1,0:T(8,128)S(1)}, f32[199,8,128]{2,1,0:T(8,128)S(1)}) custom-call(f32[128,512]{1,0:T(8,128)S(1)} %bitcast.19, f32[128,512]{1,0:T(8,128)S(1)} %bitcast.15, f32[16,512]{1,0:T(8,128)S(1)} %collective-permute-done.4.ex_rim, f32[128,512]{1,0:T(8,128)S(1)} %bitcast.27, ...), custom_call_target="tpu_custom_call" | custom-call | tf_op jit(solution)/shard_map/first_x/pallas_call | solution.py:410
  45.0 4.9 %collective-permute-done.6.other = f32[2,16,512]{2,1,0:T(8,128)S(1)} collective-permute-done((f32[2,16,512]{2,1,0:T(8,128)S(1)}, f32[2,16,512]{2,1,0:T(8,128)S(1)}, u32[]{:S(2)}, u32[]{:S(2)}) %collective-permute-start.6) | collective-permute-done | bytes 65568 | tf_op jit(solution)/shard_map/ppermute | solution.py:30
  50.2 3.1 %collective-permute-start.16 = (f32[5,16,512]{2,1,0:T(8,128)S(1)}, f32[5,16,512]{2,1,0:T(8,128)S(1)}, u32[]{:S(2)}, u32[]{:S(2)}) collective-permute-start(f32[5,16,512]{2,1,0:T(8,128)S(1)} %get-tuple-element.103.mine), channel_id=1, source_target_pairs={{0,24},{1,25},{2,26},{3,27},{4,28},{5,29},{6,30},{7,31},{8,16},{9,... | collective-permute-start | bytes 491528 | tf_op jit(solution)/shard_map/ppermute | solution.py:30
  54.3 3.0 %collective-permute-start.11 = (f32[2,16,512]{2,1,0:T(8,128)S(1)}, f32[2,16,512]{2,1,0:T(8,128)S(1)}, u32[]{:S(2)}, u32[]{:S(2)}) collective-permute-start(f32[2,16,512]{2,1,0:T(8,128)S(1)} %get-tuple-element.96.mine), channel_id=1, source_target_pairs={{0,6},{1,7},{2,4},{3,5},{4,2},{5,3},{6,0},{7,1},{8,14},{9,15},{10,... | collective-permute-start | bytes 196616 | tf_op jit(solution)/shard_map/ppermute | solution.py:30
  57.3 2.6 %collective-permute-done.11.other = f32[2,16,512]{2,1,0:T(8,128)S(1)} collective-permute-done((f32[2,16,512]{2,1,0:T(8,128)S(1)}, f32[2,16,512]{2,1,0:T(8,128)S(1)}, u32[]{:S(2)}, u32[]{:S(2)}) %collective-permute-start.11) | collective-permute-done | bytes 65568 | tf_op jit(solution)/shard_map/ppermute | solution.py:30
  62.5 1.7 %collective-permute-done.13.other = f32[2,16,512]{2,1,0:T(8,128)S(1)} collective-permute-done((f32[2,16,512]{2,1,0:T(8,128)S(1)}, f32[2,16,512]{2,1,0:T(8,128)S(1)}, u32[]{:S(2)}, u32[]{:S(2)}) %collective-permute-start.13) | collective-permute-done | bytes 65568 | tf_op jit(solution)/shard_map/ppermute | solution.py:30
  64.3 1.5 %collective-permute-start.15 = (f32[2,16,512]{2,1,0:T(8,128)S(1)}, f32[2,16,512]{2,1,0:T(8,128)S(1)}, u32[]{:S(2)}, u32[]{:S(2)}) collective-permute-start(f32[2,16,512]{2,1,0:T(8,128)S(1)} %get-tuple-element.102.mine), channel_id=1, source_target_pairs={{0,24},{1,25},{2,26},{3,27},{4,28},{5,29},{6,30},{7,31},{8,16},{9,... | collective-permute-start | bytes 196616 | tf_op jit(solution)/shard_map/ppermute | solution.py:30
  65.8 5.7 %collective-permute-start.18 = (f32[2,8,512]{2,1,0:T(8,128)S(1)}, f32[2,8,512]{2,1,0:T(8,128)S(1)}, u32[]{:S(2)}, u32[]{:S(2)}) collective-permute-start(f32[2,8,512]{2,1,0:T(8,128)S(1)} %get-tuple-element.122.mine), channel_id=1, source_target_pairs={{0,64},{32,96},{64,0},{96,32},{128,192},{160,224},{192,128},{224,1... | collective-permute-start | bytes 98312 | tf_op jit(solution)/shard_map/ppermute | solution.py:30
  71.5 1.9 %collective-permute-done.18.other = f32[2,8,512]{2,1,0:T(8,128)S(1)} collective-permute-done((f32[2,8,512]{2,1,0:T(8,128)S(1)}, f32[2,8,512]{2,1,0:T(8,128)S(1)}, u32[]{:S(2)}, u32[]{:S(2)}) %collective-permute-start.18) | collective-permute-done | bytes 32800 | tf_op jit(solution)/shard_map/ppermute | solution.py:30
  74.8 1.5 %last_x.1 = (f32[128,512]{1,0:T(8,128)}, f32[128,512]{1,0:T(8,128)}) custom-call(f32[512,128]{1,0:T(8,128)S(1)} %get-tuple-element.117.ey1, f32[128,512]{1,0:T(8,128)S(1)} %bitcast.34, f32[128,512]{1,0:T(8,128)S(1)} %bitcast.31, f32[512,128]{1,0:T(8,128)S(1)} %get-tuple-element.118.hz_u, f32[512,128]{1,0:T(8,128)S(1)} %get-tuple-element.71.ie, ...), custom_call_target="tpu_custom_call" | custom-call | tf_op jit(solution)/shard_map/last_x/pallas_call | solution.py:410
  76.3 1.6 %end_z.1 = (f32[128,512]{1,0:T(8,128)}, f32[128,512]{1,0:T(8,128)}) custom-call(f32[2,16,512]{2,1,0:T(8,128)S(1)} %get-tuple-element.105.refs_0_, f32[5,16,512]{2,1,0:T(8,128)S(1)} %get-tuple-element.106.refs_1_.pay5, f32[4,16,512]{2,1,0:T(8,128)S(1)} %get-tuple-element.92.kept.refs_2_.s0, f32[4,16,512]{2,1,0:T(8,128)S(1)} %get-tuple-element.95.kept.refs_3_.s1, ...), custom_call_target="tpu_custom_call" | custom-call | tf_op jit(solution)/shard_map/end_z/pallas_call | solution.py:410
  77.9 1.6 %collective-permute-done.19.other = f32[2,8,512]{2,1,0:T(8,128)S(1)} collective-permute-done((f32[2,8,512]{2,1,0:T(8,128)S(1)}, f32[2,8,512]{2,1,0:T(8,128)S(1)}, u32[]{:S(2)}, u32[]{:S(2)}) %collective-permute-start.19) | collective-permute-done | bytes 32800 | tf_op jit(solution)/shard_map/ppermute | solution.py:30
  (66 shorter events, 15.7 us)
Async XLA Ops:
  2.5 3.4 %collective-permute-start.7 = (f32[8,512]{1,0:T(8,128)}, f32[8,512]{1,0:T(8,128)S(1)}, u32[]{:S(2)}, u32[]{:S(2)}) collective-permute-start(f32[8,512]{1,0:T(8,128)} %get-tuple-element.89), channel_id=1, source_target_pairs={{32,0},{64,32},{96,64},{128,96},{160,128},{192,160},{224,192},{33,... | collective-permute-start | bytes 49160 | tf_op jit(solution)/shard_map/ppermute | solution.py:25
  6.5 13.9 %copy-start = (f32[16,8,512]{2,1,0:T(8,128)S(1)}, f32[16,8,512]{2,1,0:T(8,128)}, u32[]{:S(2)}) copy-start(f32[16,8,512]{2,1,0:T(8,128)} %param.9) | copy-start | bytes 786436
  6.6 13.9 %copy-start.1 = (f32[16,8,512]{2,1,0:T(8,128)S(1)}, f32[16,8,512]{2,1,0:T(8,128)}, u32[]{:S(2)}) copy-start(f32[16,8,512]{2,1,0:T(8,128)} %param.13) | copy-start | bytes 786436
  6.6 5.4 %collective-permute-start.8 = (f32[5,16,512]{2,1,0:T(8,128)S(1)}, f32[5,16,512]{2,1,0:T(8,128)S(1)}, u32[]{:S(2)}, u32[]{:S(2)}) collective-permute-start(f32[5,16,512]{2,1,0:T(8,128)S(1)} %get-tuple-element.91.mine), channel_id=1, source_target_pairs={{0,1},{1,0},{2,3},{3,2},{4,5},{5,4},{6,7},{7,6},{8,9},{9,8},{10,11... | collective-permute-start | bytes 491528 | tf_op jit(solution)/shard_map/ppermute | solution.py:30
  12.0 5.9 %collective-permute-start.10 = (f32[5,16,512]{2,1,0:T(8,128)S(1)}, f32[5,16,512]{2,1,0:T(8,128)S(1)}, u32[]{:S(2)}, u32[]{:S(2)}) collective-permute-start(f32[5,16,512]{2,1,0:T(8,128)S(1)} %get-tuple-element.94.mine), channel_id=1, source_target_pairs={{0,2},{1,3},{2,0},{3,1},{4,6},{5,7},{6,4},{7,5},{8,10},{9,11},{10,... | collective-permute-start | bytes 491528 | tf_op jit(solution)/shard_map/ppermute | solution.py:30
  13.6 6.9 %collective-permute-start = (f32[16,512]{1,0:T(8,128)S(1)}, f32[16,512]{1,0:T(8,128)S(1)}, u32[]{:S(2)}, u32[]{:S(2)}) collective-permute-start(f32[16,512]{1,0:T(8,128)S(1)} %copy-done.10), channel_id=1, source_target_pairs={{0,1},{1,2},{2,3},{3,4},{4,5},{5,6},{6,7},{7,8},{8,9},{9,10},{10,1... | collective-permute-start | bytes 98312 | tf_op jit(solution)/shard_map/ppermute | solution.py:25
  18.0 9.0 %collective-permute-start.12 = (f32[5,16,512]{2,1,0:T(8,128)S(1)}, f32[5,16,512]{2,1,0:T(8,128)S(1)}, u32[]{:S(2)}, u32[]{:S(2)}) collective-permute-start(f32[5,16,512]{2,1,0:T(8,128)S(1)} %get-tuple-element.97.mine), channel_id=1, source_target_pairs={{0,6},{1,7},{2,4},{3,5},{4,2},{5,3},{6,0},{7,1},{8,14},{9,15},{10,... | collective-permute-start | bytes 491528 | tf_op jit(solution)/shard_map/ppermute | solution.py:30
  20.7 2.1 %collective-permute-start.1 = (f32[5,8,512]{2,1,0:T(8,128)S(1)}, f32[5,8,512]{2,1,0:T(8,128)S(1)}, u32[]{:S(2)}, u32[]{:S(2)}) collective-permute-start(f32[5,8,512]{2,1,0:T(8,128)S(1)} %get-tuple-element.75.mine), channel_id=1, source_target_pairs={{0,32},{32,0},{64,96},{96,64},{128,160},{160,128},{192,224},{224,1... | collective-permute-start | bytes 245768 | tf_op jit(solution)/shard_map/ppermute | solution.py:30
  22.8 8.1 %collective-permute-start.2 = (f32[5,8,512]{2,1,0:T(8,128)S(1)}, f32[5,8,512]{2,1,0:T(8,128)S(1)}, u32[]{:S(2)}, u32[]{:S(2)}) collective-permute-start(f32[5,8,512]{2,1,0:T(8,128)S(1)} %get-tuple-element.76.mine), channel_id=1, source_target_pairs={{0,64},{32,96},{64,0},{96,32},{128,192},{160,224},{192,128},{224,1... | collective-permute-start | bytes 245768 | tf_op jit(solution)/shard_map/ppermute | solution.py:30
  27.1 9.0 %copy-start.9 = (f32[16,512]{1,0:T(8,128)S(1)}, f32[16,512]{1,0:T(8,128)}, u32[]{:S(2)}) copy-start(f32[16,512]{1,0:T(8,128)} %get-tuple-element.84) | copy-start | bytes 98308
  27.1 10.9 %copy-start.11 = (f32[8,512]{1,0:T(8,128)S(1)}, f32[8,512]{1,0:T(8,128)}, u32[]{:S(2)}) copy-start(f32[8,512]{1,0:T(8,128)} %get-tuple-element.85) | copy-start | bytes 49156
  27.1 23.1 %collective-permute-start.14 = (f32[5,16,512]{2,1,0:T(8,128)S(1)}, f32[5,16,512]{2,1,0:T(8,128)S(1)}, u32[]{:S(2)}, u32[]{:S(2)}) collective-permute-start(f32[5,16,512]{2,1,0:T(8,128)S(1)} %get-tuple-element.100.mine), channel_id=1, source_target_pairs={{0,8},{1,9},{2,10},{3,11},{4,12},{5,13},{6,14},{7,15},{8,0},{9,1},... | collective-permute-start | bytes 491528 | tf_op jit(solution)/shard_map/ppermute | solution.py:30
  31.0 13.2 %collective-permute-start.3 = (f32[5,8,512]{2,1,0:T(8,128)S(1)}, f32[5,8,512]{2,1,0:T(8,128)S(1)}, u32[]{:S(2)}, u32[]{:S(2)}) collective-permute-start(f32[5,8,512]{2,1,0:T(8,128)S(1)} %get-tuple-element.77.mine), channel_id=1, source_target_pairs={{0,192},{32,224},{64,128},{96,160},{128,64},{160,96},{192,0},{224,... | collective-permute-start | bytes 245768 | tf_op jit(solution)/shard_map/ppermute | solution.py:30
  36.1 6.7 %collective-permute-start.4 = (f32[16,512]{1,0:T(8,128)S(1)}, f32[16,512]{1,0:T(8,128)S(1)}, u32[]{:S(2)}, u32[]{:S(2)}) collective-permute-start(f32[16,512]{1,0:T(8,128)S(1)} %copy-done.9), channel_id=1, source_target_pairs={{1,0},{2,1},{3,2},{4,3},{5,4},{6,5},{7,6},{8,7},{9,8},{10,9},{11,1... | collective-permute-start | bytes 98312 | tf_op jit(solution)/shard_map/ppermute | solution.py:25
  38.0 2.1 %collective-permute-start.5 = (f32[8,512]{1,0:T(8,128)S(1)}, f32[8,512]{1,0:T(8,128)S(1)}, u32[]{:S(2)}, u32[]{:S(2)}) collective-permute-start(f32[8,512]{1,0:T(8,128)S(1)} %copy-done.11), channel_id=1, source_target_pairs={{0,32},{32,64},{64,96},{96,128},{128,160},{160,192},{192,224},{1,3... | collective-permute-start | bytes 49160 | tf_op jit(solution)/shard_map/ppermute | solution.py:25
  44.9 5.0 %collective-permute-start.6 = (f32[2,16,512]{2,1,0:T(8,128)S(1)}, f32[2,16,512]{2,1,0:T(8,128)S(1)}, u32[]{:S(2)}, u32[]{:S(2)}) collective-permute-start(f32[2,16,512]{2,1,0:T(8,128)S(1)} %get-tuple-element.88.mine), channel_id=1, source_target_pairs={{0,1},{1,0},{2,3},{3,2},{4,5},{5,4},{6,7},{7,6},{8,9},{9,8},{10,11... | collective-permute-start | bytes 196616 | tf_op jit(solution)/shard_map/ppermute | solution.py:30
  49.9 4.4 %collective-permute-start.9 = (f32[2,16,512]{2,1,0:T(8,128)S(1)}, f32[2,16,512]{2,1,0:T(8,128)S(1)}, u32[]{:S(2)}, u32[]{:S(2)}) collective-permute-start(f32[2,16,512]{2,1,0:T(8,128)S(1)} %get-tuple-element.93.mine), channel_id=1, source_target_pairs={{0,2},{1,3},{2,0},{3,1},{4,6},{5,7},{6,4},{7,5},{8,10},{9,11},{10,... | collective-permute-start | bytes 196616 | tf_op jit(solution)/shard_map/ppermute | solution.py:30
  50.2 11.0 %collective-permute-start.16 = (f32[5,16,512]{2,1,0:T(8,128)S(1)}, f32[5,16,512]{2,1,0:T(8,128)S(1)}, u32[]{:S(2)}, u32[]{:S(2)}) collective-permute-start(f32[5,16,512]{2,1,0:T(8,128)S(1)} %get-tuple-element.103.mine), channel_id=1, source_target_pairs={{0,24},{1,25},{2,26},{3,27},{4,28},{5,29},{6,30},{7,31},{8,16},{9,... | collective-permute-start | bytes 491528 | tf_op jit(solution)/shard_map/ppermute | solution.py:30
  54.3 5.6 %collective-permute-start.11 = (f32[2,16,512]{2,1,0:T(8,128)S(1)}, f32[2,16,512]{2,1,0:T(8,128)S(1)}, u32[]{:S(2)}, u32[]{:S(2)}) collective-permute-start(f32[2,16,512]{2,1,0:T(8,128)S(1)} %get-tuple-element.96.mine), channel_id=1, source_target_pairs={{0,6},{1,7},{2,4},{3,5},{4,2},{5,3},{6,0},{7,1},{8,14},{9,15},{10,... | collective-permute-start | bytes 196616 | tf_op jit(solution)/shard_map/ppermute | solution.py:30
  59.9 4.4 %collective-permute-start.13 = (f32[2,16,512]{2,1,0:T(8,128)S(1)}, f32[2,16,512]{2,1,0:T(8,128)S(1)}, u32[]{:S(2)}, u32[]{:S(2)}) collective-permute-start(f32[2,16,512]{2,1,0:T(8,128)S(1)} %get-tuple-element.99.mine), channel_id=1, source_target_pairs={{0,8},{1,9},{2,10},{3,11},{4,12},{5,13},{6,14},{7,15},{8,0},{9,1},... | collective-permute-start | bytes 196616 | tf_op jit(solution)/shard_map/ppermute | solution.py:30
  62.4 3.4 %collective-permute-start.17 = (f32[2,8,512]{2,1,0:T(8,128)S(1)}, f32[2,8,512]{2,1,0:T(8,128)S(1)}, u32[]{:S(2)}, u32[]{:S(2)}) collective-permute-start(f32[2,8,512]{2,1,0:T(8,128)S(1)} %get-tuple-element.121.mine), channel_id=1, source_target_pairs={{0,32},{32,0},{64,96},{96,64},{128,160},{160,128},{192,224},{224,1... | collective-permute-start | bytes 98312 | tf_op jit(solution)/shard_map/ppermute | solution.py:30
  64.3 12.0 %collective-permute-start.15 = (f32[2,16,512]{2,1,0:T(8,128)S(1)}, f32[2,16,512]{2,1,0:T(8,128)S(1)}, u32[]{:S(2)}, u32[]{:S(2)}) collective-permute-start(f32[2,16,512]{2,1,0:T(8,128)S(1)} %get-tuple-element.102.mine), channel_id=1, source_target_pairs={{0,24},{1,25},{2,26},{3,27},{4,28},{5,29},{6,30},{7,31},{8,16},{9,... | collective-permute-start | bytes 196616 | tf_op jit(solution)/shard_map/ppermute | solution.py:30
  65.8 7.6 %collective-permute-start.18 = (f32[2,8,512]{2,1,0:T(8,128)S(1)}, f32[2,8,512]{2,1,0:T(8,128)S(1)}, u32[]{:S(2)}, u32[]{:S(2)}) collective-permute-start(f32[2,8,512]{2,1,0:T(8,128)S(1)} %get-tuple-element.122.mine), channel_id=1, source_target_pairs={{0,64},{32,96},{64,0},{96,32},{128,192},{160,224},{192,128},{224,1... | collective-permute-start | bytes 98312 | tf_op jit(solution)/shard_map/ppermute | solution.py:30
  73.4 6.1 %collective-permute-start.19 = (f32[2,8,512]{2,1,0:T(8,128)S(1)}, f32[2,8,512]{2,1,0:T(8,128)S(1)}, u32[]{:S(2)}, u32[]{:S(2)}) collective-permute-start(f32[2,8,512]{2,1,0:T(8,128)S(1)} %get-tuple-element.123.mine), channel_id=1, source_target_pairs={{0,192},{32,224},{64,128},{96,160},{128,64},{160,96},{192,0},{224,... | collective-permute-start | bytes 98312 | tf_op jit(solution)/shard_map/ppermute | solution.py:30
  (8 other events, 35.9 us)
where the time goes:
time: 80.8 us; the launch traced here: 80.5 us
  starting transfers between devices  43.5 us (54%)
  waiting for transfers between devices  24.4 us (30%)
  Pallas kernels  11.6 us (14%)
  between operations  1.01 us (1%)
    ppermute x16, starting transfers between devices, swapped(): return lax.ppermute(array, axis, [(i, i ^ flip) for i in range(size)])  34.5 us
    ppermute x16, waiting for transfers between devices, swapped(): return lax.ppermute(array, axis, [(i, i ^ flip) for i in range(size)])  20.3 us
    pallas_call x25, Pallas kernels, call(): pl.pallas_call(kernel, out_shape=[shape(*dims) for dims in outs], in_spec...  9.85 us
    ppermute x4, starting transfers between devices, shifted(): return lax.ppermute(array, axis, pairs)  8.97 us
    ppermute x4, waiting for transfers between devices, shifted(): return lax.ppermute(array, axis, pairs)  4.02 us
    pallas_call x1, Pallas kernels, on_device(): pl.pallas_call(rims_kernel, grid=(1,), out_shape=[shape(*Z1), shape(*Y1),...  1.78 us
  transfers between devices with their start and end apart: 20, of which 12 were waited for; matrix products, arithmetic and copies ran while one was open for 0% of the time, Pallas kernels for 10%

commit v1 on v0

--- a/solution.py
+++ b/solution.py
@@ -19,10 +19,10 @@
 Z_STEPS = ((1, 0), (2, 1), (6, 2), (8, 3), (24, 4))
 
 
-def shifted(array, axis, by):
+def met(array, axis, first):
     size = lax.axis_size(axis)
-    pairs = [(i, i + by) for i in range(size) if 0 <= i + by < size]
-    return lax.ppermute(array, axis, pairs)
+    low = range(first, size - 1, 2)
+    return lax.ppermute(array, axis, [(i, i + 1) for i in low] + [(i + 1, i) for i in low])
 
 
 def swapped(array, axis, flip):
@@ -121,24 +121,70 @@
     return (lax.axis_index(axis) >> bit) & 1
 
 
-def rims_kernel(hy, ez, ex, hx, hy_top, ez_first, ex_first, hx_last):
-    ez_first[...] = ez[...]
-    hx_last[...] = hx[...]
-    for y in range(NYL):
-        hy_top[y:y + 1, :] = hy[(y + 1) * NZL - 1:(y + 1) * NZL, :]
-        ex_first[y:y + 1, :] = ex[y * NZL:y * NZL + 1, :]
-
-
-def bands_kernel(material, eps, mu, ie, ch, y_mat, z_mat, cy, cz):
+def inputs_kernel(*refs):
+    away, (eps, mu), here = refs[:7], refs[7:9], refs[9:16]
+    y_even, y_odd, z_even, z_odd, tables, eps_s, mu_s, sems = refs[16:]
+    copies = [pltpu.make_async_copy(away[i], here[i], sems.at[i]) for i in range(7)]
+    copies.append(pltpu.make_async_copy(eps, eps_s, sems.at[7]))
+    copies.append(pltpu.make_async_copy(mu, mu_s, sems.at[8]))
+    for copy in copies:
+        copy.start()
+    for copy in copies:
+        copy.wait()
+    ex, ez, hx, hy = here[0], here[2], here[3], here[4]
+
+    def fill(axis, low, high, even, odd):
+        up = (lax.axis_index(axis) & 1) == 0
+
+        @pl.when(up)
+        def _():
+            low(even)
+            high(odd)
+
+        @pl.when(jnp.logical_not(up))
+        def _():
+            high(even)
+            low(odd)
+
+    def hx_last(out):
+        out[...] = hx[plain(NYL - 1), :]
+
+    def ez_first(out):
+        out[...] = ez[plain(0), :]
+
+    def hy_last(out):
+        for y in range(NYL):
+            out[y:y + 1, :] = hy[(y + 1) * NZL - 1:(y + 1) * NZL, :]
+
+    def ex_first(out):
+        for y in range(NYL):
+            out[y:y + 1, :] = ex[y * NZL:y * NZL + 1, :]
+
+    fill("gy", hx_last, ez_first, y_even, y_odd)
+    fill("gz", hy_last, ex_first, z_even, z_odd)
+    for k in range(16):
+        tables[k:k + 1, :] = jnp.full((1, LANES), eps_s[k], F32)
+        tables[16 + k:17 + k, :] = jnp.full((1, LANES), mu_s[k], F32)
+
+
+def from_below(axis, even, odd):
+    return jnp.where(jnp.broadcast_to(lax.axis_index(axis) & 1, even.shape) == 1, even, odd)
+
+
+def from_above(axis, even, odd):
+    return jnp.where(jnp.broadcast_to(lax.axis_index(axis) & 1, even.shape) == 0, even, odd)
+
+
+def bands_kernel(material, tables, ie, ch, y_mat, z_mat, cy, cz):
+    spread = [jnp.broadcast_to(tables[k:k + 1, :], (NZL, LANES)) for k in range(32)]
     for y in range(NYL):
         for c in range(CHUNKS):
             label = material[plain(y), cut(c)]
-            e_val = jnp.full(label.shape, eps[0], F32)
-            m_val = jnp.full(label.shape, mu[0], F32)
+            e_val, m_val = spread[0], spread[16]
             for k in range(1, 16):
                 hit = label == k
-                e_val = jnp.where(hit, eps[k], e_val)
-                m_val = jnp.where(hit, mu[k], m_val)
+                e_val = jnp.where(hit, spread[k], e_val)
+                m_val = jnp.where(hit, spread[16 + k], m_val)
             ie[yrow(y, c), :] = e_val * (1.0 / courant)
             ch[yrow(y, c), :] = courant / m_val
     for c in range(CHUNKS):
@@ -170,7 +216,8 @@
     pay[1, :, cut(c)] = g
 
 
-def first_y_kernel(hz, ey, ex, hy, hy_rim, ie, ch, y_mat, cy, pay, w_out, hz_t, f_s, g_s):
+def first_y_kernel(hz, ey, ex, hy, z_even, z_odd, ie, ch, y_mat, cy, pay, w_out, hz_t, f_s, g_s, hy_rim):
+    hy_rim[...] = from_below("gz", z_even[...], z_odd[...])
     for y in range(NYL):
         r = plain(y)
         ey_r = ey[r, :]
@@ -186,10 +233,10 @@
     pay[2:5] = y_mat[...]
 
 
-def first_z_kernel(hx, ez, ez_rim, hz, ey, ie, ch, z_mat, cz, pay, w_out, hx_t, f_s, g_s):
+def first_z_kernel(hx, ez, y_even, y_odd, hz, ey, ie, ch, z_mat, cz, pay, w_out, hx_t, f_s, g_s):
     for y in range(NYL):
         r = plain(y)
-        up = ez[plain(y + 1), :] if y < NYL - 1 else ez_rim[...]
+        up = ez[plain(y + 1), :] if y < NYL - 1 else from_above("gy", y_even[...], y_odd[...])
         ht = hx[r, :] - wide(ch, y) * (up - ez[r, :])
         hz_r = hz[r, :]
         put_wide(hx_t, y, ht)
@@ -200,29 +247,43 @@
     pay[2:5] = z_mat[...]
 
 
-def merge_all(lower, upper, pay, save):
+def merge_all(axis, top, lower, upper, pay, save, edge):
     stamp, (p, q, inv) = merge_mat((lower[2], lower[3], lower[4]), (upper[2], upper[3], upper[4]))
     (f, g), w = merge_rhs((lower[0], lower[1]), (upper[0], upper[1]), p, q)
-    pay[0], pay[1], pay[2], pay[3], pay[4] = f, g, *stamp
     save[0], save[1], save[2], save[3] = p, q, inv, w
-
-
-def merge_kernel(axis, bit, mine, other, pay, save):
+    if top is None:
+        pay[0], pay[1], pay[2], pay[3], pay[4] = f, g, *stamp
+        return
+    ga, b, gc = stamp
+    share = 1.0 / (ga + b)
+    reach = b * share
+    high = jnp.broadcast_to(bit_of(axis, top), f.shape) == 1
+    pay[0] = jnp.where(high, f, g + reach * f)
+    pay[1] = jnp.where(high, ga + b, gc + reach * ga)
+    edge[0], edge[1], edge[2] = reach, share, f
+
+
+def merge_kernel(axis, bit, top, mine, other, pay, save, edge=None):
     side = bit_of(axis, bit)
 
     @pl.when(side == 0)
     def _():
-        merge_all(mine, other, pay, save)
+        merge_all(axis, top, mine, other, pay, save, edge)
 
     @pl.when(side == 1)
     def _():
-        merge_all(other, mine, pay, save)
-
-
-def again_all(lower, upper, kept, pay, w_out):
+        merge_all(axis, top, other, mine, pay, save, edge)
+
+
+def again_all(axis, top, lower, upper, kept, edge, pay, w_out, f_out):
     (f, g), w = merge_rhs((lower[0], lower[1]), (upper[0], upper[1]), kept[0], kept[1])
-    pay[0], pay[1] = f, g
     w_out[...] = w
+    if top is None:
+        pay[0], pay[1] = f, g
+        return
+    high = jnp.broadcast_to(bit_of(axis, top), f.shape) == 1
+    pay[...] = jnp.where(high, f, g + edge[0] * f)
+    f_out[...] = f
 
 
 def again_kernel(axis, bit, mine, other, kept, pay, w_out):
@@ -230,16 +291,29 @@
 
     @pl.when(side == 0)
     def _():
-        again_all(mine, other, kept, pay, w_out)
+        again_all(axis, None, mine, other, kept, None, pay, w_out, None)
 
     @pl.when(side == 1)
     def _():
-        again_all(other, mine, kept, pay, w_out)
-
-
-def ends_of(axis, levels, sources, f, total):
-    x_lo = f / total
-    x_hi = jnp.zeros_like(x_lo)
+        again_all(axis, None, other, mine, kept, None, pay, w_out, None)
+
+
+def again_top_kernel(axis, bit, top, mine, other, kept, edge, pay, w_out, f_out):
+    side = bit_of(axis, bit)
+
+    @pl.when(side == 0)
+    def _():
+        again_all(axis, top, mine, other, kept, edge, pay, w_out, f_out)
+
+    @pl.when(side == 1)
+    def _():
+        again_all(axis, top, other, mine, kept, edge, pay, w_out, f_out)
+
+
+def ends_of(axis, x_meet, reach, share, f, levels, sources):
+    high = jnp.broadcast_to(bit_of(axis, len(levels)), x_meet.shape) == 1
+    x_lo = jnp.where(high, x_meet, share * f + reach * x_meet)
+    x_hi = jnp.where(high, 0.0, x_meet)
     for bit in reversed(range(len(levels))):
         kept = levels[bit]
         x_mid = kept[0] * x_lo + kept[1] * x_hi + kept[2] * sources[bit]
@@ -248,6 +322,11 @@
     return x_lo, x_hi
 
 
+def first_ends(axis, mine, other, edge, levels, inv):
+    inv[...] = 1.0 / (mine[1] + other[1])
+    return ends_of(axis, (mine[0] + other[0]) * inv[...], edge[0], edge[1], edge[2], levels, [s[3] for s in levels])
+
+
 def down_local(rows, count, c, x_lo, x_hi, coef, w_of, put):
     def get(j, k):
         return coef[j * (count - 1) + k, :, cut(c)]
@@ -258,10 +337,9 @@
     tree_down(0, count, x_lo[:, cut(c)], x_hi[:, cut(c)], get, source, put)
 
 
-def mid_y_kernel(pay3, s0, s1, s2, cy, w_y, hz_t, hy, hy_u, ex, ie, ch, cz,
-                 hz_u, pay, w_out, lo_s, hi_s, f_s, g_s):
-    levels = (s0, s1, s2)
-    lo_s[...], hi_s[...] = ends_of("gy", levels, [s[3] for s in levels], pay3[0], pay3[2] + pay3[3])
+def mid_y_kernel(mine, other, edge, s0, s1, cy, w_y, hz_t, hy, hy_u, ex, ie, ch, cz,
+                 hz_u, pay, w_out, inv, lo_s, hi_s, f_s, g_s):
+    lo_s[...], hi_s[...] = first_ends("gy", mine, other, edge, (s0, s1), inv)
     for c in range(CHUNKS):
 
         def put(y, x, x_next):
@@ -275,10 +353,9 @@
         up_local(zrow, NZL, c, f_s, g_s, cz, w_out, pay)
 
 
-def mid_z_kernel(pay5, s0, s1, s2, s3, s4, cz, w_z, hx_t, hx, ez1, ez, ie, ch, cy,
-                 ey1, hx_u, pay, w_out, lo_s, hi_s, f_s, g_s):
-    levels = (s0, s1, s2, s3, s4)
-    lo_s[...], hi_s[...] = ends_of("gz", levels, [s[3] for s in levels], pay5[0], pay5[2] + pay5[3])
+def mid_z_kernel(mine, other, edge, s0, s1, s2, s3, cz, w_z, hx_t, hx, ez1, ez, ie, ch, cy,
+                 ey1, hx_u, pay, w_out, inv, lo_s, hi_s, f_s, g_s):
+    lo_s[...], hi_s[...] = first_ends("gz", mine, other, edge, (s0, s1, s2, s3), inv)
     for c in range(CHUNKS):
 
         def put(z, x, x_next):
@@ -297,10 +374,12 @@
 
 
 def end_kernel(axis, rows, count, steps, *refs):
-    pay, total = refs[0], refs[1]
-    levels, sources = refs[2:2 + steps], refs[2 + steps:2 + 2 * steps]
-    coef, w_of, h_u, ch, e_new, h_new, lo_s, hi_s, e_s, h_s = refs[2 + 2 * steps:]
-    lo_s[...], hi_s[...] = ends_of(axis, levels, [s[...] for s in sources], pay[0], total[2] + total[3])
+    mine, other, inv, edge, f = refs[:5]
+    levels, sources = refs[5:5 + steps], refs[5 + steps:5 + 2 * steps]
+    coef, w_of, h_u, ch, e_new, h_new, done, lo_s, hi_s, e_s, h_s = refs[5 + 2 * steps:]
+    done[...] = jnp.zeros_like(done)
+    lo_s[...], hi_s[...] = ends_of(axis, (mine[...] + other[...]) * inv[...], edge[0], edge[1], f[...], levels,
+                                   [s[...] for s in sources])
     for c in range(CHUNKS):
 
         def put(i, x, x_next):
@@ -370,14 +449,15 @@
         x_out[:, cut(c)] = r_t[cut(c), :].T
 
 
-def first_x_kernel(hy, ex, ex_rim, hx, hx_rim, ez, ie, ch, ez1, hy_u, cx, r_t, e_t, h_t, w_s, rhs):
+def first_x_kernel(hy, ex, z_even, z_odd, hx, y_even, y_odd, ez, ie, ch, ez1, hy_u, cx, r_t, e_t, h_t, w_s, rhs, ex_rim):
+    ex_rim[...] = from_above("gz", z_even[...], z_odd[...])
     for y in range(NYL):
         r = plain(y)
         ex_r = ex[r, :]
         z_of = lax.broadcasted_iota(jnp.int32, ex_r.shape, 0)
         up = jnp.where(z_of == NZL - 1, jnp.broadcast_to(ex_rim[y:y + 1, :], ex_r.shape), pltpu.roll(ex_r, NZL - 1, 0))
         ht = hy[r, :] - wide(ch, y) * (up - ex_r)
-        low = hx[plain(y - 1), :] if y > 0 else hx_rim[...]
+        low = hx[plain(y - 1), :] if y > 0 else from_below("gy", y_even[...], y_odd[...])
         put_wide(hy_u, y, ht)
         rhs[r, :] = wide(ie, y) * ez[r, :] + (ht - prev_x(ht)) - (hx[r, :] - low)
     x_solve(rhs, ie, ch, cx, True, ez1, r_t, e_t, h_t, w_s)
@@ -386,7 +466,8 @@
         put_wide(hy_u, y, wide(hy_u, y) + 2.0 * (wide(ch, y) * (next_x(x) - x)))
 
 
-def last_x_kernel(ey1, ey, hz, hz_u, ie, ch, cx, ey_new, hz_new, r_t, w_s, rhs):
+def last_x_kernel(ey1, ey, hz, hz_u, ie, ch, cx, ey_new, hz_new, done, r_t, w_s, rhs):
+    done[...] = jnp.zeros_like(done)
     for y in range(NYL):
         r = plain(y)
         s = hz[r, :] - wide(hz_u, y)
@@ -399,23 +480,34 @@
 
 
 VM = pl.BlockSpec(memory_space=pltpu.VMEM)
-SM = pl.BlockSpec(memory_space=pltpu.SMEM)
 
 
 def shape(*dims):
     return jax.ShapeDtypeStruct(dims, F32)
 
 
-def call(kernel, args, outs, scratch=(), specs=None, name=None, flops=100000):
-    return pl.pallas_call(
-        kernel,
-        out_shape=[shape(*dims) for dims in outs],
-        in_specs=specs or [VM] * len(args),
-        out_specs=[VM] * len(outs),
-        scratch_shapes=[pltpu.VMEM(dims, F32) for dims in scratch],
-        compiler_params=pltpu.CompilerParams(vmem_limit_bytes=40 * 1024 * 1024),
-        name=name,
-    )(*args)
+class Order:
+    def __init__(self):
+        self.last = None
+
+    def __call__(self, kernel, args, outs, scratch=(), specs=None, after=(), name=None):
+        after = list(after) + ([] if self.last is None else [self.last])
+        count = len(args)
+
+        def body(*refs):
+            kernel(*refs[:count], *refs[count + len(after):])
+
+        results = pl.pallas_call(
+            body,
+            out_shape=[shape(*dims) for dims in outs],
+            in_specs=(specs or [VM] * count) + [pl.BlockSpec(memory_space=pl.ANY)] * len(after),
+            out_specs=[VM] * len(outs),
+            scratch_shapes=[pltpu.VMEM(dims, F32) for dims in scratch],
+            compiler_params=pltpu.CompilerParams(vmem_limit_bytes=16 * 1024 * 1024),
+            name=name,
+        )(*args, *after)
+        self.last = results[-1]
+        return results
 
 
 FIELD = (ROWS, NX)
@@ -426,78 +518,89 @@
 def on_device(ex, ey, ez, hx, hy, hz, material, eps_table, mu_table):
     ex, ey, ez, hx, hy, hz, material = (a.reshape(FIELD) for a in (ex, ey, ez, hx, hy, hz, material))
 
-    whole = pl.BlockSpec(FIELD, lambda i: (0, 0))
-    hy_top, ez_first, ex_first, hx_last = pl.pallas_call(
-        rims_kernel,
-        grid=(1,),
-        out_shape=[shape(*Z1), shape(*Y1), shape(*Z1), shape(*Y1)],
-        in_specs=[whole, pl.BlockSpec(Y1, lambda i: (0, 0)), whole, pl.BlockSpec(Y1, lambda i: (NYL - 1, 0))],
-        out_specs=[pl.BlockSpec(Z1, lambda i: (0, 0)), pl.BlockSpec(Y1, lambda i: (0, 0)),
-                   pl.BlockSpec(Z1, lambda i: (0, 0)), pl.BlockSpec(Y1, lambda i: (0, 0))],
-        name="rims",
-    )(hy, ez, ex, hx)
-    hy_rim = shifted(hy_top, "gz", 1)
-    ez_rim = shifted(ez_first, "gy", -1)
-    ex_rim = shifted(ex_first, "gz", -1)
-    hx_rim = shifted(hx_last, "gy", 1)
+    call = Order()
+
+    inputs = (ex, ey, ez, hx, hy, hz, material)
+    ex, ey, ez, hx, hy, hz, material, y_even, y_odd, z_even, z_odd, tables = pl.pallas_call(
+        inputs_kernel,
+        out_shape=[jax.ShapeDtypeStruct(FIELD, a.dtype) for a in inputs]
+        + [shape(*Y1), shape(*Y1), shape(*Z1), shape(*Z1), shape(32, LANES)],
+        in_specs=[pl.BlockSpec(memory_space=pltpu.HBM)] * 9,
+        out_specs=[VM] * 12,
+        scratch_shapes=[pltpu.SMEM((16,), F32), pltpu.SMEM((16,), F32), pltpu.SemaphoreType.DMA((9,))],
+        compiler_params=pltpu.CompilerParams(vmem_limit_bytes=52 * 1024 * 1024),
+        name="inputs",
+    )(*inputs, eps_table, mu_table)
+    y_even, z_even = met(y_even, "gy", 0), met(z_even, "gz", 0)
+    y_odd, z_odd = met(y_odd, "gy", 1), met(z_odd, "gz", 1)
 
     ie, ch, y_mat, z_mat, cy, cz = call(
-        bands_kernel, (material, eps_table, mu_table),
-        (PACKED, PACKED, (3,) + Y1, (3,) + Z1, (45,) + Y1, (21,) + Z1), specs=[VM, SM, SM], name="bands")
-
-    pay_y, w_y, hz_t = call(first_y_kernel, (hz, ey, ex, hy, hy_rim, ie, ch, y_mat, cy),
-                            ((5,) + Y1, (15,) + Y1, PACKED), (PACKED, PACKED), name="first_y")
-    pay_z, w_z, hx_t = call(first_z_kernel, (hx, ez, ez_rim, hz, ey, ie, ch, z_mat, cz),
-                            ((5,) + Z1, (7,) + Z1, PACKED), (PACKED, PACKED), name="first_z")
-
-    def merge(pay, axis, step, plane):
+        bands_kernel, (material, tables),
+        (PACKED, PACKED, (3,) + Y1, (3,) + Z1, (45,) + Y1, (21,) + Z1), name="bands")
+
+    pay_z, w_z, hx_t = call(first_z_kernel, (hx, ez, y_even, y_odd, hz, ey, ie, ch, z_mat, cz),
+                            ((5,) + Z1, (7,) + Z1, PACKED), (PACKED, PACKED), after=(z_even, z_odd), name="first_z")
+    pay_y, w_y, hz_t = call(first_y_kernel, (hz, ey, ex, hy, z_even, z_odd, ie, ch, y_mat, cy),
+                            ((5,) + Y1, (15,) + Y1, PACKED), (PACKED, PACKED, Z1), name="first_y")
+
+    def merge(pay, axis, step, plane, saved, top=None):
         flip, bit = step
         other = swapped(pay, axis, flip)
-        return call(functools.partial(merge_kernel, axis, bit), (pay, other), ((5,) + plane, (4,) + plane), name="merge")
-
-    def again(pay, axis, step, plane, kept):
+        kernel = functools.partial(merge_kernel, axis, bit, top)
+        if top is None:
+            pay, kept = call(kernel, (pay, other), ((5,) + plane, (4,) + plane), name="merge_" + axis)
+            saved.append(kept)
+            return pay
+        pay, kept, edge = call(kernel, (pay, other), ((2,) + plane, (4,) + plane, (3,) + plane), name="merge_" + axis)
+        saved.append(kept)
+        return pay, edge
+
+    def again(pay, axis, step, plane, kept, sources, top=None, edge=None):
         flip, bit = step
         other = swapped(pay, axis, flip)
-        return call(functools.partial(again_kernel, axis, bit), (pay, other, kept), ((2,) + plane, plane), name="again")
-
-    ez1, hy_u, cx = call(first_x_kernel, (hy, ex, ex_rim, hx, hx_rim, ez, ie, ch),
+        if top is None:
+            pay, w = call(functools.partial(again_kernel, axis, bit), (pay, other, kept), ((2,) + plane, plane),
+                          name="again_" + axis)
+            sources.append(w)
+            return pay
+        pay, w, f = call(functools.partial(again_top_kernel, axis, bit, top), (pay, other, kept, edge),
+                         (plane, plane, plane), name="again_" + axis)
+        sources.append(w)
+        return pay, f
+
+    save_z, save_y, from_z, from_y = [], [], [], []
+    pay_z = merge(pay_z, "gz", Z_STEPS[0], Z1, save_z)
+    pay_y = merge(pay_y, "gy", Y_STEPS[0], Y1, save_y)
+    ez1, hy_u, cx = call(first_x_kernel, (hy, ex, z_even, z_odd, hx, y_even, y_odd, ez, ie, ch),
                          (FIELD, PACKED, (3 * (RUN + 2) + 1, 8, LANES)),
-                         ((NX, LANES), (NX, LANES), (NX, LANES), (RUN + 2, 8, LANES), FIELD), name="first_x")
-
-    save_y = []
-    for step in Y_STEPS:
-        pay_y, kept = merge(pay_y, "gy", step, Y1)
-        save_y.append(kept)
-    hz_u, pay_z2, w_z2 = call(
-        mid_y_kernel, (pay_y, *save_y, cy, w_y, hz_t, hy, hy_u, ex, ie, ch, cz),
-        (PACKED, (2,) + Z1, (7,) + Z1), (Y1, Y1, PACKED, PACKED), name="mid_y")
-
-    save_z = []
-    for step in Z_STEPS:
-        pay_z, kept = merge(pay_z, "gz", step, Z1)
-        save_z.append(kept)
-    ey1, hx_u, pay_y2, w_y2 = call(
-        mid_z_kernel, (pay_z, *save_z, cz, w_z, hx_t, hx, ez1, ez, ie, ch, cy),
-        (PACKED, PACKED, (2,) + Y1, (15,) + Y1), (Z1, Z1, PACKED, PACKED), name="mid_z")
-
-    from_z = []
-    for step, kept in zip(Z_STEPS, save_z):
-        pay_z2, w = again(pay_z2, "gz", step, Z1, kept)
-        from_z.append(w)
-    ex_new, hy_new = call(
-        functools.partial(end_kernel, "gz", zrow, NZL, 5), (pay_z2, pay_z, *save_z, *from_z, cz, w_z2, hy_u, ch),
-        (FIELD, FIELD), (Z1, Z1, PACKED, PACKED), name="end_z")
-
-    from_y = []
-    for step, kept in zip(Y_STEPS, save_y):
-        pay_y2, w = again(pay_y2, "gy", step, Y1, kept)
-        from_y.append(w)
-    ez_new, hx_new = call(
-        functools.partial(end_kernel, "gy", yrow, NYL, 3), (pay_y2, pay_y, *save_y, *from_y, cy, w_y2, hx_u, ch),
-        (FIELD, FIELD), (Y1, Y1, PACKED, PACKED), name="end_y")
-
-    ey_new, hz_new = call(last_x_kernel, (ey1, ey, hz, hz_u, ie, ch, cx), (FIELD, FIELD),
-                          ((NX, LANES), (RUN + 2, 8, LANES), FIELD), name="last_x")
+                         ((NX, LANES), (NX, LANES), (NX, LANES), (RUN + 2, 8, LANES), FIELD, Z1), name="first_x")
+    pay_z = merge(pay_z, "gz", Z_STEPS[1], Z1, save_z)
+    pay_y, edge_y = merge(pay_y, "gy", Y_STEPS[1], Y1, save_y, Y_STEPS[2][1])
+    pay_z = merge(pay_z, "gz", Z_STEPS[2], Z1, save_z)
+    hz_u, pay_z2, w_z2, inv_y = call(
+        mid_y_kernel, (pay_y, swapped(pay_y, "gy", Y_STEPS[2][0]), edge_y, *save_y, cy, w_y, hz_t, hy, hy_u, ex, ie, ch, cz),
+        (PACKED, (2,) + Z1, (7,) + Z1, Y1), (Y1, Y1, PACKED, PACKED), name="mid_y")
+    pay_z, edge_z = merge(pay_z, "gz", Z_STEPS[3], Z1, save_z, Z_STEPS[4][1])
+    pay_z2 = again(pay_z2, "gz", Z_STEPS[0], Z1, save_z[0], from_z)
+    ey1, hx_u, pay_y2, w_y2, inv_z = call(
+        mid_z_kernel, (pay_z, swapped(pay_z, "gz", Z_STEPS[4][0]), edge_z, *save_z, cz, w_z, hx_t, hx, ez1, ez, ie, ch, cy),
+        (PACKED, PACKED, (2,) + Y1, (15,) + Y1, Z1), (Z1, Z1, PACKED, PACKED), name="mid_z")
+    pay_z2 = again(pay_z2, "gz", Z_STEPS[1], Z1, save_z[1], from_z)
+    pay_y2 = again(pay_y2, "gy", Y_STEPS[0], Y1, save_y[0], from_y)
+    pay_z2 = again(pay_z2, "gz", Z_STEPS[2], Z1, save_z[2], from_z)
+    pay_y2, f_y = again(pay_y2, "gy", Y_STEPS[1], Y1, save_y[1], from_y, Y_STEPS[2][1], edge_y)
+    pay_z2, f_z = again(pay_z2, "gz", Z_STEPS[3], Z1, save_z[3], from_z, Z_STEPS[4][1], edge_z)
+    mark = (8, LANES)
+    ey_new, hz_new, _ = call(last_x_kernel, (ey1, ey, hz, hz_u, ie, ch, cx), (FIELD, FIELD, mark),
+                             ((NX, LANES), (RUN + 2, 8, LANES), FIELD), name="last_x")
+    ez_new, hx_new, _ = call(
+        functools.partial(end_kernel, "gy", yrow, NYL, 2),
+        (pay_y2, swapped(pay_y2, "gy", Y_STEPS[2][0]), inv_y, edge_y, f_y, *save_y, *from_y, cy, w_y2, hx_u, ch),
+        (FIELD, FIELD, mark), (Y1, Y1, PACKED, PACKED), name="end_y")
+    ex_new, hy_new, _ = call(
+        functools.partial(end_kernel, "gz", zrow, NZL, 4),
+        (pay_z2, swapped(pay_z2, "gz", Z_STEPS[4][0]), inv_z, edge_z, f_z, *save_z, *from_z, cz, w_z2, hy_u, ch),
+        (FIELD, FIELD, mark), (Z1, Z1, PACKED, PACKED), name="end_z")
 
     return tuple(a.reshape(NYL, NZL, NX) for a in (ex_new, ey_new, ez_new, hx_new, hy_new, hz_new))
 

time: 80.8 us -> 77.3 us (0.957)
  starting transfers between devices: 43.5 us -> 37.9 us
  waiting for transfers between devices: 24.4 us -> 26.1 us
    ppermute x16, waiting for transfers between devices: 20.3 us -> 24 us  [swapped(): return lax.ppermute(array, axis, [(i, i ^ flip) for i in range(size)])]
    ppermute x4, starting transfers between devices: 8.97 us -> 5.69 us  [met(): lax.ppermute(array, axis, [(i, i + 1) for i in low] + [(i + 1, i) for i i...]
    ppermute x16, starting transfers between devices: 34.5 us -> 32.2 us  [swapped(): return lax.ppermute(array, axis, [(i, i ^ flip) for i in range(size)])]
    ppermute x4, waiting for transfers between devices: 4.02 us -> 2.07 us  [met(): lax.ppermute(array, axis, [(i, i + 1) for i in low] + [(i + 1, i) for i i...]
    pallas_call x26 -> x22, Pallas kernels: 11.6 us -> 10.8 us  [the longest x21 9.18 us: __call__(): pl.pallas_call(body, out_shape=[shape(*dims) for dims in outs], in_specs=...]
  transfers between devices with their start and end apart: 20 -> 20, of which waited for: 12 -> 13; matrix products, arithmetic and copies ran while one was open for 0% -> 0% of each run, Pallas kernels for 10% -> 9%
where the time goes in v1:
time: 77.3 us; the launch traced here: 76.3 us
  starting transfers between devices  37.9 us (49%)
  waiting for transfers between devices  26.1 us (34%)
  Pallas kernels  10.8 us (14%)
  between operations  0.89 us (1%)
    ppermute x16, starting transfers between devices, swapped(): return lax.ppermute(array, axis, [(i, i ^ flip) for i in range(size)])  32.2 us
    ppermute x16, waiting for transfers between devices, swapped(): return lax.ppermute(array, axis, [(i, i ^ flip) for i in range(size)])  24 us
    pallas_call x21, Pallas kernels, __call__(): pl.pallas_call(body, out_shape=[shape(*dims) for dims in outs], in_specs=...  9.18 us
    ppermute x4, starting transfers between devices, met(): lax.ppermute(array, axis, [(i, i + 1) for i in low] + [(i + 1, i) for i i...  5.69 us
    ppermute x4, waiting for transfers between devices, met(): lax.ppermute(array, axis, [(i, i + 1) for i in low] + [(i + 1, i) for i i...  2.07 us
    pallas_call x1, Pallas kernels, on_device(): pl.pallas_call(inputs_kernel, out_shape=[jax.ShapeDtypeStruct(FIELD, a.dt...  1.58 us
  transfers between devices with their start and end apart: 20, of which 13 were waited for; matrix products, arithmetic and copies ran while one was open for 0% of the time, Pallas kernels for 9%

profile of v1, /device:TPU:32, one launch (start us, length us, event | category | flops | bytes accessed | tf_op | source)
XLA Modules:
  0.0 76.3 jit_solution(4456437507307983172)
XLA Ops:
  1.3 1.6 %inputs.1 = (f32[128,512]{1,0:T(8,128)S(1)}, f32[128,512]{1,0:T(8,128)S(1)}, f32[128,512]{1,0:T(8,128)S(1)}, f32[128,512]{1,0:T(8,128)S(1)}, f32[128,512]{1,0:T(...) custom-call(f32[128,512]{1,0:T(8,128)} %bitcast.13, ...), custom_call_target="tpu_custom_call" | custom-call | tf_op jit(solution)/shard_map/inputs/pallas_call | solution.py:524
  2.9 1.9 %collective-permute-start = (f32[16,512]{1,0:T(8,128)S(1)}, f32[16,512]{1,0:T(8,128)S(1)}, u32[]{:S(2)}, u32[]{:S(2)}) collective-permute-start(f32[16,512]{1,0:T(8,128)S(1)} %get-tuple-element.82), channel_id=1, source_target_pairs={{0,1},{2,3},{4,5},{6,7},{8,9},{10,11},{12,13},{14,15},{16,17},{18,... | collective-permute-start | bytes 98312 | tf_op jit(solution)/shard_map/ppermute | solution.py:25
  4.8 3.0 %collective-permute-start.1 = (f32[16,512]{1,0:T(8,128)S(1)}, f32[16,512]{1,0:T(8,128)S(1)}, u32[]{:S(2)}, u32[]{:S(2)}) collective-permute-start(f32[16,512]{1,0:T(8,128)S(1)} %get-tuple-element.83), channel_id=1, source_target_pairs={{1,2},{3,4},{5,6},{7,8},{9,10},{11,12},{13,14},{15,16},{17,18},{19... | collective-permute-start | bytes 98312 | tf_op jit(solution)/shard_map/ppermute | solution.py:25
  9.5 2.1 %collective-permute-done.1.refs_11_.refs_5_.refs_3_ = f32[16,512]{1,0:T(8,128)S(1)} collective-permute-done((f32[16,512]{1,0:T(8,128)S(1)}, f32[16,512]{1,0:T(8,128)S(1)}, u32[]{:S(2)}, u32[]{:S(2)}) %collective-permute-start.1) | collective-permute-done | bytes 32800 | tf_op jit(solution)/shard_map/ppermute | solution.py:25
  12.5 5.1 %collective-permute-done.5.refs_1_ = f32[5,16,512]{2,1,0:T(8,128)S(1)} collective-permute-done((f32[5,16,512]{2,1,0:T(8,128)S(1)}, f32[5,16,512]{2,1,0:T(8,128)S(1)}, u32[]{:S(2)}, u32[]{:S(2)}) %collective-permute-start.5) | collective-permute-done | bytes 163872 | tf_op jit(solution)/shard_map/ppermute | solution.py:30
  17.7 3.2 %collective-permute-start.4 = (f32[5,8,512]{2,1,0:T(8,128)S(1)}, f32[5,8,512]{2,1,0:T(8,128)S(1)}, u32[]{:S(2)}, u32[]{:S(2)}) collective-permute-start(f32[5,8,512]{2,1,0:T(8,128)S(1)} %get-tuple-element.97.refs_0_), channel_id=1, source_target_pairs={{0,32},{32,0},{64,96},{96,64},{128,160},{160,128},{192,224},{224,1... | collective-permute-start | bytes 245768 | tf_op jit(solution)/shard_map/ppermute | solution.py:30
  21.8 1.5 %first_x.1 = (f32[128,512]{1,0:T(8,128)S(1)}, f32[512,128]{1,0:T(8,128)S(1)}, f32[199,8,128]{2,1,0:T(8,128)S(1)}) custom-call(f32[128,512]{1,0:T(8,128)S(1)} %get-tuple-element.81.refs_3_.refs_0_.refs_8_, f32[128,512]{1,0:T(8,128)S(1)} %get-tuple-element.80.refs_2_.refs_1_.refs_10_, f32[16,512]{1,0:T(8,128)S(1)} %collective-permute-done.refs_10_.refs_4_.refs_2_, ...), custom_call_target="tpu_custom_call" | custom-call | tf_op jit(solution)/shard_map/first_x/pallas_call | solution.py:500
  23.6 3.8 %collective-permute-start.9 = (f32[5,16,512]{2,1,0:T(8,128)S(1)}, f32[5,16,512]{2,1,0:T(8,128)S(1)}, u32[]{:S(2)}, u32[]{:S(2)}) collective-permute-start(f32[5,16,512]{2,1,0:T(8,128)S(1)} %get-tuple-element.111.refs_0_), channel_id=1, source_target_pairs={{0,6},{1,7},{2,4},{3,5},{4,2},{5,3},{6,0},{7,1},{8,14},{9,15},{10,... | collective-permute-start | bytes 491528 | tf_op jit(solution)/shard_map/ppermute | solution.py:30
  27.4 6.5 %collective-permute-start.6 = (f32[5,8,512]{2,1,0:T(8,128)S(1)}, f32[5,8,512]{2,1,0:T(8,128)S(1)}, u32[]{:S(2)}, u32[]{:S(2)}) collective-permute-start(f32[5,8,512]{2,1,0:T(8,128)S(1)} %get-tuple-element.101.refs_0_), channel_id=1, source_target_pairs={{0,64},{32,96},{64,0},{96,32},{128,192},{160,224},{192,128},{224,1... | collective-permute-start | bytes 245768 | tf_op jit(solution)/shard_map/ppermute | solution.py:30
  33.9 2.8 %collective-permute-done.6.refs_1_ = f32[5,8,512]{2,1,0:T(8,128)S(1)} collective-permute-done((f32[5,8,512]{2,1,0:T(8,128)S(1)}, f32[5,8,512]{2,1,0:T(8,128)S(1)}, u32[]{:S(2)}, u32[]{:S(2)}) %collective-permute-start.6) | collective-permute-done | bytes 81952 | tf_op jit(solution)/shard_map/ppermute | solution.py:30
  36.8 1.7 %collective-permute-start.11 = (f32[5,16,512]{2,1,0:T(8,128)S(1)}, f32[5,16,512]{2,1,0:T(8,128)S(1)}, u32[]{:S(2)}, u32[]{:S(2)}) collective-permute-start(f32[5,16,512]{2,1,0:T(8,128)S(1)} %get-tuple-element.114.refs_0_), channel_id=1, source_target_pairs={{0,8},{1,9},{2,10},{3,11},{4,12},{5,13},{6,14},{7,15},{8,0},{9,1},... | collective-permute-start | bytes 491528 | tf_op jit(solution)/shard_map/ppermute | solution.py:30
  38.4 3.2 %collective-permute-start.8 = (f32[2,8,512]{2,1,0:T(8,128)S(1)}, f32[2,8,512]{2,1,0:T(8,128)S(1)}, u32[]{:S(2)}, u32[]{:S(2)}) collective-permute-start(f32[2,8,512]{2,1,0:T(8,128)S(1)} %get-tuple-element.106.refs_0_), channel_id=1, source_target_pairs={{0,192},{32,224},{64,128},{96,160},{128,64},{160,96},{192,0},{224,... | collective-permute-start | bytes 98312 | tf_op jit(solution)/shard_map/ppermute | solution.py:30
  41.6 2.8 %collective-permute-done.8.refs_1_ = f32[2,8,512]{2,1,0:T(8,128)S(1)} collective-permute-done((f32[2,8,512]{2,1,0:T(8,128)S(1)}, f32[2,8,512]{2,1,0:T(8,128)S(1)}, u32[]{:S(2)}, u32[]{:S(2)}) %collective-permute-start.8) | collective-permute-done | bytes 32800 | tf_op jit(solution)/shard_map/ppermute | solution.py:30
  45.1 1.5 %collective-permute-start.10 = (f32[2,16,512]{2,1,0:T(8,128)S(1)}, f32[2,16,512]{2,1,0:T(8,128)S(1)}, u32[]{:S(2)}, u32[]{:S(2)}) collective-permute-start(f32[2,16,512]{2,1,0:T(8,128)S(1)} %get-tuple-element.113.refs_0_), channel_id=1, source_target_pairs={{0,1},{1,0},{2,3},{3,2},{4,5},{5,4},{6,7},{7,6},{8,9},{9,8},{10,11... | collective-permute-start | bytes 196616 | tf_op jit(solution)/shard_map/ppermute | solution.py:30
  46.7 2.0 %collective-permute-start.13 = (f32[2,16,512]{2,1,0:T(8,128)S(1)}, f32[2,16,512]{2,1,0:T(8,128)S(1)}, u32[]{:S(2)}, u32[]{:S(2)}) collective-permute-start(f32[2,16,512]{2,1,0:T(8,128)S(1)} %get-tuple-element.118.refs_0_), channel_id=1, source_target_pairs={{0,24},{1,25},{2,26},{3,27},{4,28},{5,29},{6,30},{7,31},{8,16},{9,... | collective-permute-start | bytes 196616 | tf_op jit(solution)/shard_map/ppermute | solution.py:30
  49.8 2.5 %collective-permute-done.13.refs_1_ = f32[2,16,512]{2,1,0:T(8,128)S(1)} collective-permute-done((f32[2,16,512]{2,1,0:T(8,128)S(1)}, f32[2,16,512]{2,1,0:T(8,128)S(1)}, u32[]{:S(2)}, u32[]{:S(2)}) %collective-permute-start.13) | collective-permute-done | bytes 65568 | tf_op jit(solution)/shard_map/ppermute | solution.py:30
  56.7 2.9 %collective-permute-done.14.refs_1_ = f32[2,16,512]{2,1,0:T(8,128)S(1)} collective-permute-done((f32[2,16,512]{2,1,0:T(8,128)S(1)}, f32[2,16,512]{2,1,0:T(8,128)S(1)}, u32[]{:S(2)}, u32[]{:S(2)}) %collective-permute-start.14) | collective-permute-done | bytes 65568 | tf_op jit(solution)/shard_map/ppermute | solution.py:30
  60.2 3.4 %collective-permute-start.17 = (f32[2,8,512]{2,1,0:T(8,128)S(1)}, f32[2,8,512]{2,1,0:T(8,128)S(1)}, u32[]{:S(2)}, u32[]{:S(2)}) collective-permute-start(f32[2,8,512]{2,1,0:T(8,128)S(1)} %get-tuple-element.129.refs_0_), channel_id=1, source_target_pairs={{0,64},{32,96},{64,0},{96,32},{128,192},{160,224},{192,128},{224,1... | collective-permute-start | bytes 98312 | tf_op jit(solution)/shard_map/ppermute | solution.py:30
  63.5 1.9 %collective-permute-done.17.refs_1_ = f32[2,8,512]{2,1,0:T(8,128)S(1)} collective-permute-done((f32[2,8,512]{2,1,0:T(8,128)S(1)}, f32[2,8,512]{2,1,0:T(8,128)S(1)}, u32[]{:S(2)}, u32[]{:S(2)}) %collective-permute-start.17) | collective-permute-done | bytes 32800 | tf_op jit(solution)/shard_map/ppermute | solution.py:30
  65.5 2.4 %collective-permute-start.18 = (f32[16,512]{1,0:T(8,128)S(1)}, f32[16,512]{1,0:T(8,128)S(1)}, u32[]{:S(2)}, u32[]{:S(2)}) collective-permute-start(f32[16,512]{1,0:T(8,128)S(1)} %get-tuple-element.132.refs_0_), channel_id=1, source_target_pairs={{0,24},{1,25},{2,26},{3,27},{4,28},{5,29},{6,30},{7,31},{8,16},{9,... | collective-permute-start | bytes 98312 | tf_op jit(solution)/shard_map/ppermute | solution.py:30
  67.9 2.2 %collective-permute-start.19 = (f32[8,512]{1,0:T(8,128)S(1)}, f32[8,512]{1,0:T(8,128)S(1)}, u32[]{:S(2)}, u32[]{:S(2)}) collective-permute-start(f32[8,512]{1,0:T(8,128)S(1)} %get-tuple-element.136.refs_0_), channel_id=1, source_target_pairs={{0,192},{32,224},{64,128},{96,160},{128,64},{160,96},{192,0},{224,... | collective-permute-start | bytes 49160 | tf_op jit(solution)/shard_map/ppermute | solution.py:30
  70.1 1.6 %last_x.1 = (f32[128,512]{1,0:T(8,128)}, f32[128,512]{1,0:T(8,128)}, f32[8,128]{1,0:T(8,128)S(1)}) custom-call(f32[512,128]{1,0:T(8,128)S(1)} %get-tuple-element.140.refs_0_, f32[128,512]{1,0:T(8,128)S(1)} %get-tuple-element.79.refs_5_.refs_1_, f32[128,512]{1,0:T(8,128)S(1)} %get-tuple-element.78.refs_4_.refs_0_.refs_2_, ...), custom_call_target="tpu_custom_call" | custom-call | tf_op jit(solution)/shard_map/last_x/pallas_call | solution.py:500
  71.7 2.1 %collective-permute-done.19.refs_1_ = f32[8,512]{1,0:T(8,128)S(1)} collective-permute-done((f32[8,512]{1,0:T(8,128)S(1)}, f32[8,512]{1,0:T(8,128)S(1)}, u32[]{:S(2)}, u32[]{:S(2)}) %collective-permute-start.19) | collective-permute-done | bytes 16416 | tf_op jit(solution)/shard_map/ppermute | solution.py:30
  74.7 1.6 %end_z.1 = (f32[128,512]{1,0:T(8,128)}, f32[128,512]{1,0:T(8,128)}, f32[8,128]{1,0:T(8,128)}) custom-call(f32[16,512]{1,0:T(8,128)S(1)} %get-tuple-element.132.refs_0_, f32[16,512]{1,0:T(8,128)S(1)} %collective-permute-done.18.refs_1_, f32[16,512]{1,0:T(8,128)S(1)} %get-tuple-element.123.refs_3_.refs_2_, ...), custom_call_target="tpu_custom_call" | custom-call | tf_op jit(solution)/shard_map/end_z/pallas_call | solution.py:500
  (42 shorter events, 12.4 us)
Async XLA Ops:
  0.6 0.7 copy-start
  0.6 0.7 copy-start.1
  2.9 6.6 %collective-permute-start = (f32[16,512]{1,0:T(8,128)S(1)}, f32[16,512]{1,0:T(8,128)S(1)}, u32[]{:S(2)}, u32[]{:S(2)}) collective-permute-start(f32[16,512]{1,0:T(8,128)S(1)} %get-tuple-element.82), channel_id=1, source_target_pairs={{0,1},{2,3},{4,5},{6,7},{8,9},{10,11},{12,13},{14,15},{16,17},{18,... | collective-permute-start | bytes 98312 | tf_op jit(solution)/shard_map/ppermute | solution.py:25
  4.8 6.7 %collective-permute-start.1 = (f32[16,512]{1,0:T(8,128)S(1)}, f32[16,512]{1,0:T(8,128)S(1)}, u32[]{:S(2)}, u32[]{:S(2)}) collective-permute-start(f32[16,512]{1,0:T(8,128)S(1)} %get-tuple-element.83), channel_id=1, source_target_pairs={{1,2},{3,4},{5,6},{7,8},{9,10},{11,12},{13,14},{15,16},{17,18},{19... | collective-permute-start | bytes 98312 | tf_op jit(solution)/shard_map/ppermute | solution.py:25
  7.8 1.6 %collective-permute-start.2 = (f32[8,512]{1,0:T(8,128)S(1)}, f32[8,512]{1,0:T(8,128)S(1)}, u32[]{:S(2)}, u32[]{:S(2)}) collective-permute-start(f32[8,512]{1,0:T(8,128)S(1)} %get-tuple-element.92), channel_id=1, source_target_pairs={{0,32},{64,96},{128,160},{192,224},{32,0},{96,64},{160,128},{224,1... | collective-permute-start | bytes 49160 | tf_op jit(solution)/shard_map/ppermute | solution.py:25
  7.9 1.5 %collective-permute-start.3 = (f32[8,512]{1,0:T(8,128)S(1)}, f32[8,512]{1,0:T(8,128)S(1)}, u32[]{:S(2)}, u32[]{:S(2)}) collective-permute-start(f32[8,512]{1,0:T(8,128)S(1)} %get-tuple-element.93), channel_id=1, source_target_pairs={{32,64},{96,128},{160,192},{64,32},{128,96},{192,160},{33,65},{97,... | collective-permute-start | bytes 49160 | tf_op jit(solution)/shard_map/ppermute | solution.py:25
  12.2 5.4 %collective-permute-start.5 = (f32[5,16,512]{2,1,0:T(8,128)S(1)}, f32[5,16,512]{2,1,0:T(8,128)S(1)}, u32[]{:S(2)}, u32[]{:S(2)}) collective-permute-start(f32[5,16,512]{2,1,0:T(8,128)S(1)} %get-tuple-element.98.refs_0_), channel_id=1, source_target_pairs={{0,1},{1,0},{2,3},{3,2},{4,5},{5,4},{6,7},{7,6},{8,9},{9,8},{10,11... | collective-permute-start | bytes 491528 | tf_op jit(solution)/shard_map/ppermute | solution.py:30
  17.6 5.9 %collective-permute-start.7 = (f32[5,16,512]{2,1,0:T(8,128)S(1)}, f32[5,16,512]{2,1,0:T(8,128)S(1)}, u32[]{:S(2)}, u32[]{:S(2)}) collective-permute-start(f32[5,16,512]{2,1,0:T(8,128)S(1)} %get-tuple-element.102.refs_0_), channel_id=1, source_target_pairs={{0,2},{1,3},{2,0},{3,1},{4,6},{5,7},{6,4},{7,5},{8,10},{9,11},{10,... | collective-permute-start | bytes 491528 | tf_op jit(solution)/shard_map/ppermute | solution.py:30
  17.7 4.1 %collective-permute-start.4 = (f32[5,8,512]{2,1,0:T(8,128)S(1)}, f32[5,8,512]{2,1,0:T(8,128)S(1)}, u32[]{:S(2)}, u32[]{:S(2)}) collective-permute-start(f32[5,8,512]{2,1,0:T(8,128)S(1)} %get-tuple-element.97.refs_0_), channel_id=1, source_target_pairs={{0,32},{32,0},{64,96},{96,64},{128,160},{160,128},{192,224},{224,1... | collective-permute-start | bytes 245768 | tf_op jit(solution)/shard_map/ppermute | solution.py:30
  23.6 13.1 %collective-permute-start.9 = (f32[5,16,512]{2,1,0:T(8,128)S(1)}, f32[5,16,512]{2,1,0:T(8,128)S(1)}, u32[]{:S(2)}, u32[]{:S(2)}) collective-permute-start(f32[5,16,512]{2,1,0:T(8,128)S(1)} %get-tuple-element.111.refs_0_), channel_id=1, source_target_pairs={{0,6},{1,7},{2,4},{3,5},{4,2},{5,3},{6,0},{7,1},{8,14},{9,15},{10,... | collective-permute-start | bytes 491528 | tf_op jit(solution)/shard_map/ppermute | solution.py:30
  27.4 9.2 %collective-permute-start.6 = (f32[5,8,512]{2,1,0:T(8,128)S(1)}, f32[5,8,512]{2,1,0:T(8,128)S(1)}, u32[]{:S(2)}, u32[]{:S(2)}) collective-permute-start(f32[5,8,512]{2,1,0:T(8,128)S(1)} %get-tuple-element.101.refs_0_), channel_id=1, source_target_pairs={{0,64},{32,96},{64,0},{96,32},{128,192},{160,224},{192,128},{224,1... | collective-permute-start | bytes 245768 | tf_op jit(solution)/shard_map/ppermute | solution.py:30
  36.8 9.9 %collective-permute-start.11 = (f32[5,16,512]{2,1,0:T(8,128)S(1)}, f32[5,16,512]{2,1,0:T(8,128)S(1)}, u32[]{:S(2)}, u32[]{:S(2)}) collective-permute-start(f32[5,16,512]{2,1,0:T(8,128)S(1)} %get-tuple-element.114.refs_0_), channel_id=1, source_target_pairs={{0,8},{1,9},{2,10},{3,11},{4,12},{5,13},{6,14},{7,15},{8,0},{9,1},... | collective-permute-start | bytes 491528 | tf_op jit(solution)/shard_map/ppermute | solution.py:30
  38.4 6.0 %collective-permute-start.8 = (f32[2,8,512]{2,1,0:T(8,128)S(1)}, f32[2,8,512]{2,1,0:T(8,128)S(1)}, u32[]{:S(2)}, u32[]{:S(2)}) collective-permute-start(f32[2,8,512]{2,1,0:T(8,128)S(1)} %get-tuple-element.106.refs_0_), channel_id=1, source_target_pairs={{0,192},{32,224},{64,128},{96,160},{128,64},{160,96},{192,0},{224,... | collective-permute-start | bytes 98312 | tf_op jit(solution)/shard_map/ppermute | solution.py:30
  45.1 4.4 %collective-permute-start.10 = (f32[2,16,512]{2,1,0:T(8,128)S(1)}, f32[2,16,512]{2,1,0:T(8,128)S(1)}, u32[]{:S(2)}, u32[]{:S(2)}) collective-permute-start(f32[2,16,512]{2,1,0:T(8,128)S(1)} %get-tuple-element.113.refs_0_), channel_id=1, source_target_pairs={{0,1},{1,0},{2,3},{3,2},{4,5},{5,4},{6,7},{7,6},{8,9},{9,8},{10,11... | collective-permute-start | bytes 196616 | tf_op jit(solution)/shard_map/ppermute | solution.py:30
  46.7 5.6 %collective-permute-start.13 = (f32[2,16,512]{2,1,0:T(8,128)S(1)}, f32[2,16,512]{2,1,0:T(8,128)S(1)}, u32[]{:S(2)}, u32[]{:S(2)}) collective-permute-start(f32[2,16,512]{2,1,0:T(8,128)S(1)} %get-tuple-element.118.refs_0_), channel_id=1, source_target_pairs={{0,24},{1,25},{2,26},{3,27},{4,28},{5,29},{6,30},{7,31},{8,16},{9,... | collective-permute-start | bytes 196616 | tf_op jit(solution)/shard_map/ppermute | solution.py:30
  49.5 4.5 %collective-permute-start.12 = (f32[2,16,512]{2,1,0:T(8,128)S(1)}, f32[2,16,512]{2,1,0:T(8,128)S(1)}, u32[]{:S(2)}, u32[]{:S(2)}) collective-permute-start(f32[2,16,512]{2,1,0:T(8,128)S(1)} %get-tuple-element.117.refs_0_), channel_id=1, source_target_pairs={{0,2},{1,3},{2,0},{3,1},{4,6},{5,7},{6,4},{7,5},{8,10},{9,11},{10,... | collective-permute-start | bytes 196616 | tf_op jit(solution)/shard_map/ppermute | solution.py:30
  54.0 5.6 %collective-permute-start.14 = (f32[2,16,512]{2,1,0:T(8,128)S(1)}, f32[2,16,512]{2,1,0:T(8,128)S(1)}, u32[]{:S(2)}, u32[]{:S(2)}) collective-permute-start(f32[2,16,512]{2,1,0:T(8,128)S(1)} %get-tuple-element.124.refs_0_), channel_id=1, source_target_pairs={{0,6},{1,7},{2,4},{3,5},{4,2},{5,3},{6,0},{7,1},{8,14},{9,15},{10,... | collective-permute-start | bytes 196616 | tf_op jit(solution)/shard_map/ppermute | solution.py:30
  55.5 1.2 %collective-permute-start.15 = (f32[2,8,512]{2,1,0:T(8,128)S(1)}, f32[2,8,512]{2,1,0:T(8,128)S(1)}, u32[]{:S(2)}, u32[]{:S(2)}) collective-permute-start(f32[2,8,512]{2,1,0:T(8,128)S(1)} %get-tuple-element.125.refs_0_), channel_id=1, source_target_pairs={{0,32},{32,0},{64,96},{96,64},{128,160},{160,128},{192,224},{224,1... | collective-permute-start | bytes 98312 | tf_op jit(solution)/shard_map/ppermute | solution.py:30
  59.6 5.8 %collective-permute-start.16 = (f32[2,16,512]{2,1,0:T(8,128)S(1)}, f32[2,16,512]{2,1,0:T(8,128)S(1)}, u32[]{:S(2)}, u32[]{:S(2)}) collective-permute-start(f32[2,16,512]{2,1,0:T(8,128)S(1)} %get-tuple-element.128.refs_0_), channel_id=1, source_target_pairs={{0,8},{1,9},{2,10},{3,11},{4,12},{5,13},{6,14},{7,15},{8,0},{9,1},... | collective-permute-start | bytes 196616 | tf_op jit(solution)/shard_map/ppermute | solution.py:30
  60.2 5.3 %collective-permute-start.17 = (f32[2,8,512]{2,1,0:T(8,128)S(1)}, f32[2,8,512]{2,1,0:T(8,128)S(1)}, u32[]{:S(2)}, u32[]{:S(2)}) collective-permute-start(f32[2,8,512]{2,1,0:T(8,128)S(1)} %get-tuple-element.129.refs_0_), channel_id=1, source_target_pairs={{0,64},{32,96},{64,0},{96,32},{128,192},{160,224},{192,128},{224,1... | collective-permute-start | bytes 98312 | tf_op jit(solution)/shard_map/ppermute | solution.py:30
  65.5 9.2 %collective-permute-start.18 = (f32[16,512]{1,0:T(8,128)S(1)}, f32[16,512]{1,0:T(8,128)S(1)}, u32[]{:S(2)}, u32[]{:S(2)}) collective-permute-start(f32[16,512]{1,0:T(8,128)S(1)} %get-tuple-element.132.refs_0_), channel_id=1, source_target_pairs={{0,24},{1,25},{2,26},{3,27},{4,28},{5,29},{6,30},{7,31},{8,16},{9,... | collective-permute-start | bytes 98312 | tf_op jit(solution)/shard_map/ppermute | solution.py:30
  67.9 5.8 %collective-permute-start.19 = (f32[8,512]{1,0:T(8,128)S(1)}, f32[8,512]{1,0:T(8,128)S(1)}, u32[]{:S(2)}, u32[]{:S(2)}) collective-permute-start(f32[8,512]{1,0:T(8,128)S(1)} %get-tuple-element.136.refs_0_), channel_id=1, source_target_pairs={{0,192},{32,224},{64,128},{96,160},{128,64},{160,96},{192,0},{224,... | collective-permute-start | bytes 49160 | tf_op jit(solution)/shard_map/ppermute | solution.py:30

commit v2 on v1

--- a/solution.py
+++ b/solution.py
@@ -538,10 +538,10 @@
         bands_kernel, (material, tables),
         (PACKED, PACKED, (3,) + Y1, (3,) + Z1, (45,) + Y1, (21,) + Z1), name="bands")
 
+    pay_y, w_y, hz_t = call(first_y_kernel, (hz, ey, ex, hy, z_even, z_odd, ie, ch, y_mat, cy),
+                            ((5,) + Y1, (15,) + Y1, PACKED), (PACKED, PACKED, Z1), after=(y_even, y_odd), name="first_y")
     pay_z, w_z, hx_t = call(first_z_kernel, (hx, ez, y_even, y_odd, hz, ey, ie, ch, z_mat, cz),
-                            ((5,) + Z1, (7,) + Z1, PACKED), (PACKED, PACKED), after=(z_even, z_odd), name="first_z")
-    pay_y, w_y, hz_t = call(first_y_kernel, (hz, ey, ex, hy, z_even, z_odd, ie, ch, y_mat, cy),
-                            ((5,) + Y1, (15,) + Y1, PACKED), (PACKED, PACKED, Z1), name="first_y")
+                            ((5,) + Z1, (7,) + Z1, PACKED), (PACKED, PACKED), name="first_z")
 
     def merge(pay, axis, step, plane, saved, top=None):
         flip, bit = step
@@ -569,38 +569,38 @@
         return pay, f
 
     save_z, save_y, from_z, from_y = [], [], [], []
+    pay_y = merge(pay_y, "gy", Y_STEPS[0], Y1, save_y)
     pay_z = merge(pay_z, "gz", Z_STEPS[0], Z1, save_z)
-    pay_y = merge(pay_y, "gy", Y_STEPS[0], Y1, save_y)
     ez1, hy_u, cx = call(first_x_kernel, (hy, ex, z_even, z_odd, hx, y_even, y_odd, ez, ie, ch),
                          (FIELD, PACKED, (3 * (RUN + 2) + 1, 8, LANES)),
                          ((NX, LANES), (NX, LANES), (NX, LANES), (RUN + 2, 8, LANES), FIELD, Z1), name="first_x")
+    pay_y, edge_y = merge(pay_y, "gy", Y_STEPS[1], Y1, save_y, Y_STEPS[2][1])
     pay_z = merge(pay_z, "gz", Z_STEPS[1], Z1, save_z)
-    pay_y, edge_y = merge(pay_y, "gy", Y_STEPS[1], Y1, save_y, Y_STEPS[2][1])
-    pay_z = merge(pay_z, "gz", Z_STEPS[2], Z1, save_z)
     hz_u, pay_z2, w_z2, inv_y = call(
         mid_y_kernel, (pay_y, swapped(pay_y, "gy", Y_STEPS[2][0]), edge_y, *save_y, cy, w_y, hz_t, hy, hy_u, ex, ie, ch, cz),
         (PACKED, (2,) + Z1, (7,) + Z1, Y1), (Y1, Y1, PACKED, PACKED), name="mid_y")
+    pay_z = merge(pay_z, "gz", Z_STEPS[2], Z1, save_z)
+    pay_z2 = again(pay_z2, "gz", Z_STEPS[0], Z1, save_z[0], from_z)
     pay_z, edge_z = merge(pay_z, "gz", Z_STEPS[3], Z1, save_z, Z_STEPS[4][1])
-    pay_z2 = again(pay_z2, "gz", Z_STEPS[0], Z1, save_z[0], from_z)
+    pay_z2 = again(pay_z2, "gz", Z_STEPS[1], Z1, save_z[1], from_z)
     ey1, hx_u, pay_y2, w_y2, inv_z = call(
         mid_z_kernel, (pay_z, swapped(pay_z, "gz", Z_STEPS[4][0]), edge_z, *save_z, cz, w_z, hx_t, hx, ez1, ez, ie, ch, cy),
         (PACKED, PACKED, (2,) + Y1, (15,) + Y1, Z1), (Z1, Z1, PACKED, PACKED), name="mid_z")
-    pay_z2 = again(pay_z2, "gz", Z_STEPS[1], Z1, save_z[1], from_z)
     pay_y2 = again(pay_y2, "gy", Y_STEPS[0], Y1, save_y[0], from_y)
     pay_z2 = again(pay_z2, "gz", Z_STEPS[2], Z1, save_z[2], from_z)
+    pay_z2, f_z = again(pay_z2, "gz", Z_STEPS[3], Z1, save_z[3], from_z, Z_STEPS[4][1], edge_z)
     pay_y2, f_y = again(pay_y2, "gy", Y_STEPS[1], Y1, save_y[1], from_y, Y_STEPS[2][1], edge_y)
-    pay_z2, f_z = again(pay_z2, "gz", Z_STEPS[3], Z1, save_z[3], from_z, Z_STEPS[4][1], edge_z)
     mark = (8, LANES)
     ey_new, hz_new, _ = call(last_x_kernel, (ey1, ey, hz, hz_u, ie, ch, cx), (FIELD, FIELD, mark),
                              ((NX, LANES), (RUN + 2, 8, LANES), FIELD), name="last_x")
+    ex_new, hy_new, _ = call(
+        functools.partial(end_kernel, "gz", zrow, NZL, 4),
+        (pay_z2, swapped(pay_z2, "gz", Z_STEPS[4][0]), inv_z, edge_z, f_z, *save_z, *from_z, cz, w_z2, hy_u, ch),
+        (FIELD, FIELD, mark), (Z1, Z1, PACKED, PACKED), name="end_z")
     ez_new, hx_new, _ = call(
         functools.partial(end_kernel, "gy", yrow, NYL, 2),
         (pay_y2, swapped(pay_y2, "gy", Y_STEPS[2][0]), inv_y, edge_y, f_y, *save_y, *from_y, cy, w_y2, hx_u, ch),
         (FIELD, FIELD, mark), (Y1, Y1, PACKED, PACKED), name="end_y")
-    ex_new, hy_new, _ = call(
-        functools.partial(end_kernel, "gz", zrow, NZL, 4),
-        (pay_z2, swapped(pay_z2, "gz", Z_STEPS[4][0]), inv_z, edge_z, f_z, *save_z, *from_z, cz, w_z2, hy_u, ch),
-        (FIELD, FIELD, mark), (Z1, Z1, PACKED, PACKED), name="end_z")
 
     return tuple(a.reshape(NYL, NZL, NX) for a in (ex_new, ey_new, ez_new, hx_new, hy_new, hz_new))
 

time: 77.3 us -> 69.3 us (0.90)
  waiting for transfers between devices: 26.1 us -> 15.4 us
  starting transfers between devices: 37.9 us -> 41.4 us
    ppermute x16, waiting for transfers between devices: 24 us -> 13.4 us  [swapped(): return lax.ppermute(array, axis, [(i, i ^ flip) for i in range(size)])]
    ppermute x16, starting transfers between devices: 32.2 us -> 35.7 us  [swapped(): return lax.ppermute(array, axis, [(i, i ^ flip) for i in range(size)])]
  transfers between devices with their start and end apart: 20 -> 20, of which waited for: 13 -> 11; matrix products, arithmetic and copies ran while one was open for 0% -> 0% of each run, Pallas kernels for 9% -> 10%
where the time goes in v2:
time: 69.3 us; the launch traced here: 69.1 us
  starting transfers between devices  41.4 us (60%)
  waiting for transfers between devices  15.4 us (22%)
  Pallas kernels  10.7 us (15%)
  between operations  0.88 us (1%)
    ppermute x16, starting transfers between devices, swapped(): return lax.ppermute(array, axis, [(i, i ^ flip) for i in range(size)])  35.7 us
    ppermute x16, waiting for transfers between devices, swapped(): return lax.ppermute(array, axis, [(i, i ^ flip) for i in range(size)])  13.4 us
    pallas_call x21, Pallas kernels, __call__(): pl.pallas_call(body, out_shape=[shape(*dims) for dims in outs], in_specs=...  9.15 us
    ppermute x4, starting transfers between devices, met(): lax.ppermute(array, axis, [(i, i + 1) for i in low] + [(i + 1, i) for i i...  5.69 us
    ppermute x4, waiting for transfers between devices, met(): lax.ppermute(array, axis, [(i, i + 1) for i in low] + [(i + 1, i) for i i...  2.07 us
    pallas_call x1, Pallas kernels, on_device(): pl.pallas_call(inputs_kernel, out_shape=[jax.ShapeDtypeStruct(FIELD, a.dt...  1.58 us
  transfers between devices with their start and end apart: 20, of which 11 were waited for; matrix products, arithmetic and copies ran while one was open for 0% of the time, Pallas kernels for 10%

profile of v2, /device:TPU:32, one launch (start us, length us, event | category | flops | bytes accessed | tf_op | source)
XLA Modules:
  0.0 69.1 jit_solution(7293482752008380007)
XLA Ops:
  1.3 1.6 %inputs.1 = (f32[128,512]{1,0:T(8,128)S(1)}, f32[128,512]{1,0:T(8,128)S(1)}, f32[128,512]{1,0:T(8,128)S(1)}, f32[128,512]{1,0:T(8,128)S(1)}, f32[128,512]{1,0:T(...) custom-call(f32[128,512]{1,0:T(8,128)} %bitcast.13, ...), custom_call_target="tpu_custom_call" | custom-call | tf_op jit(solution)/shard_map/inputs/pallas_call | solution.py:524
  2.9 1.9 %collective-permute-start = (f32[16,512]{1,0:T(8,128)S(1)}, f32[16,512]{1,0:T(8,128)S(1)}, u32[]{:S(2)}, u32[]{:S(2)}) collective-permute-start(f32[16,512]{1,0:T(8,128)S(1)} %get-tuple-element.82), channel_id=1, source_target_pairs={{0,1},{2,3},{4,5},{6,7},{8,9},{10,11},{12,13},{14,15},{16,17},{18,... | collective-permute-start | bytes 98312 | tf_op jit(solution)/shard_map/ppermute | solution.py:25
  4.8 3.0 %collective-permute-start.1 = (f32[16,512]{1,0:T(8,128)S(1)}, f32[16,512]{1,0:T(8,128)S(1)}, u32[]{:S(2)}, u32[]{:S(2)}) collective-permute-start(f32[16,512]{1,0:T(8,128)S(1)} %get-tuple-element.83), channel_id=1, source_target_pairs={{1,2},{3,4},{5,6},{7,8},{9,10},{11,12},{13,14},{15,16},{17,18},{19... | collective-permute-start | bytes 98312 | tf_op jit(solution)/shard_map/ppermute | solution.py:25
  9.5 2.1 %collective-permute-done.1.refs_5_.refs_3_ = f32[16,512]{1,0:T(8,128)S(1)} collective-permute-done((f32[16,512]{1,0:T(8,128)S(1)}, f32[16,512]{1,0:T(8,128)S(1)}, u32[]{:S(2)}, u32[]{:S(2)}) %collective-permute-start.1) | collective-permute-done | bytes 32800 | tf_op jit(solution)/shard_map/ppermute | solution.py:25
  12.5 3.4 %collective-permute-start.4 = (f32[5,8,512]{2,1,0:T(8,128)S(1)}, f32[5,8,512]{2,1,0:T(8,128)S(1)}, u32[]{:S(2)}, u32[]{:S(2)}) collective-permute-start(f32[5,8,512]{2,1,0:T(8,128)S(1)} %get-tuple-element.93.refs_0_), channel_id=1, source_target_pairs={{0,32},{32,0},{64,96},{96,64},{128,160},{160,128},{192,224},{224,1... | collective-permute-start | bytes 245768 | tf_op jit(solution)/shard_map/ppermute | solution.py:30
  18.6 7.6 %collective-permute-start.5 = (f32[5,8,512]{2,1,0:T(8,128)S(1)}, f32[5,8,512]{2,1,0:T(8,128)S(1)}, u32[]{:S(2)}, u32[]{:S(2)}) collective-permute-start(f32[5,8,512]{2,1,0:T(8,128)S(1)} %get-tuple-element.99.refs_0_), channel_id=1, source_target_pairs={{0,64},{32,96},{64,0},{96,32},{128,192},{160,224},{192,128},{224,1... | collective-permute-start | bytes 245768 | tf_op jit(solution)/shard_map/ppermute | solution.py:30
  26.1 1.5 %first_x.1 = (f32[128,512]{1,0:T(8,128)S(1)}, f32[512,128]{1,0:T(8,128)S(1)}, f32[199,8,128]{2,1,0:T(8,128)S(1)}) custom-call(f32[128,512]{1,0:T(8,128)S(1)} %get-tuple-element.81.refs_3_.refs_0_.refs_8_, f32[128,512]{1,0:T(8,128)S(1)} %get-tuple-element.80.refs_2_.refs_1_.refs_10_, f32[16,512]{1,0:T(8,128)S(1)} %collective-permute-done.refs_4_.refs_2_, ...), custom_call_target="tpu_custom_call" | custom-call | tf_op jit(solution)/shard_map/first_x/pallas_call | solution.py:500
  27.6 1.8 %collective-permute-done.5.refs_1_ = f32[5,8,512]{2,1,0:T(8,128)S(1)} collective-permute-done((f32[5,8,512]{2,1,0:T(8,128)S(1)}, f32[5,8,512]{2,1,0:T(8,128)S(1)}, u32[]{:S(2)}, u32[]{:S(2)}) %collective-permute-start.5) | collective-permute-done | bytes 81952 | tf_op jit(solution)/shard_map/ppermute | solution.py:30
  29.5 1.9 %collective-permute-start.10 = (f32[5,16,512]{2,1,0:T(8,128)S(1)}, f32[5,16,512]{2,1,0:T(8,128)S(1)}, u32[]{:S(2)}, u32[]{:S(2)}) collective-permute-start(f32[5,16,512]{2,1,0:T(8,128)S(1)} %get-tuple-element.112.refs_0_), channel_id=1, source_target_pairs={{0,6},{1,7},{2,4},{3,5},{4,2},{5,3},{6,0},{7,1},{8,14},{9,15},{10,... | collective-permute-start | bytes 491528 | tf_op jit(solution)/shard_map/ppermute | solution.py:30
  31.4 4.0 %collective-permute-start.7 = (f32[2,8,512]{2,1,0:T(8,128)S(1)}, f32[2,8,512]{2,1,0:T(8,128)S(1)}, u32[]{:S(2)}, u32[]{:S(2)}) collective-permute-start(f32[2,8,512]{2,1,0:T(8,128)S(1)} %get-tuple-element.104.refs_0_), channel_id=1, source_target_pairs={{0,192},{32,224},{64,128},{96,160},{128,64},{160,96},{192,0},{224,... | collective-permute-start | bytes 98312 | tf_op jit(solution)/shard_map/ppermute | solution.py:30
  35.4 2.1 %collective-permute-done.7.refs_1_ = f32[2,8,512]{2,1,0:T(8,128)S(1)} collective-permute-done((f32[2,8,512]{2,1,0:T(8,128)S(1)}, f32[2,8,512]{2,1,0:T(8,128)S(1)}, u32[]{:S(2)}, u32[]{:S(2)}) %collective-permute-start.7) | collective-permute-done | bytes 32800 | tf_op jit(solution)/shard_map/ppermute | solution.py:30
  38.2 1.7 %collective-permute-start.12 = (f32[5,16,512]{2,1,0:T(8,128)S(1)}, f32[5,16,512]{2,1,0:T(8,128)S(1)}, u32[]{:S(2)}, u32[]{:S(2)}) collective-permute-start(f32[5,16,512]{2,1,0:T(8,128)S(1)} %get-tuple-element.116.refs_0_), channel_id=1, source_target_pairs={{0,8},{1,9},{2,10},{3,11},{4,12},{5,13},{6,14},{7,15},{8,0},{9,1},... | collective-permute-start | bytes 491528 | tf_op jit(solution)/shard_map/ppermute | solution.py:30
  39.8 1.3 %collective-permute-start.9 = (f32[2,16,512]{2,1,0:T(8,128)S(1)}, f32[2,16,512]{2,1,0:T(8,128)S(1)}, u32[]{:S(2)}, u32[]{:S(2)}) collective-permute-start(f32[2,16,512]{2,1,0:T(8,128)S(1)} %get-tuple-element.111.refs_0_), channel_id=1, source_target_pairs={{0,1},{1,0},{2,3},{3,2},{4,5},{5,4},{6,7},{7,6},{8,9},{9,8},{10,11... | collective-permute-start | bytes 196616 | tf_op jit(solution)/shard_map/ppermute | solution.py:30
  41.1 3.0 %collective-permute-done.9.refs_1_ = f32[2,16,512]{2,1,0:T(8,128)S(1)} collective-permute-done((f32[2,16,512]{2,1,0:T(8,128)S(1)}, f32[2,16,512]{2,1,0:T(8,128)S(1)}, u32[]{:S(2)}, u32[]{:S(2)}) %collective-permute-start.9) | collective-permute-done | bytes 65568 | tf_op jit(solution)/shard_map/ppermute | solution.py:30
  45.2 2.0 %collective-permute-start.14 = (f32[2,16,512]{2,1,0:T(8,128)S(1)}, f32[2,16,512]{2,1,0:T(8,128)S(1)}, u32[]{:S(2)}, u32[]{:S(2)}) collective-permute-start(f32[2,16,512]{2,1,0:T(8,128)S(1)} %get-tuple-element.120.refs_0_), channel_id=1, source_target_pairs={{0,24},{1,25},{2,26},{3,27},{4,28},{5,29},{6,30},{7,31},{8,16},{9,... | collective-permute-start | bytes 196616 | tf_op jit(solution)/shard_map/ppermute | solution.py:30
  47.1 1.4 %collective-permute-done.11.refs_1_ = f32[2,16,512]{2,1,0:T(8,128)S(1)} collective-permute-done((f32[2,16,512]{2,1,0:T(8,128)S(1)}, f32[2,16,512]{2,1,0:T(8,128)S(1)}, u32[]{:S(2)}, u32[]{:S(2)}) %collective-permute-start.11) | collective-permute-done | bytes 65568 | tf_op jit(solution)/shard_map/ppermute | solution.py:30
  48.5 1.8 %collective-permute-start.13 = (f32[2,16,512]{2,1,0:T(8,128)S(1)}, f32[2,16,512]{2,1,0:T(8,128)S(1)}, u32[]{:S(2)}, u32[]{:S(2)}) collective-permute-start(f32[2,16,512]{2,1,0:T(8,128)S(1)} %get-tuple-element.119.refs_0_), channel_id=1, source_target_pairs={{0,6},{1,7},{2,4},{3,5},{4,2},{5,3},{6,0},{7,1},{8,14},{9,15},{10,... | collective-permute-start | bytes 196616 | tf_op jit(solution)/shard_map/ppermute | solution.py:30
  51.8 1.2 %collective-permute-done.15.refs_1_ = f32[2,8,512]{2,1,0:T(8,128)S(1)} collective-permute-done((f32[2,8,512]{2,1,0:T(8,128)S(1)}, f32[2,8,512]{2,1,0:T(8,128)S(1)}, u32[]{:S(2)}, u32[]{:S(2)}) %collective-permute-start.15) | collective-permute-done | bytes 32800 | tf_op jit(solution)/shard_map/ppermute | solution.py:30
  53.0 1.3 %collective-permute-done.13.refs_1_ = f32[2,16,512]{2,1,0:T(8,128)S(1)} collective-permute-done((f32[2,16,512]{2,1,0:T(8,128)S(1)}, f32[2,16,512]{2,1,0:T(8,128)S(1)}, u32[]{:S(2)}, u32[]{:S(2)}) %collective-permute-start.13) | collective-permute-done | bytes 65568 | tf_op jit(solution)/shard_map/ppermute | solution.py:30
  54.8 3.4 %collective-permute-start.18 = (f32[2,8,512]{2,1,0:T(8,128)S(1)}, f32[2,8,512]{2,1,0:T(8,128)S(1)}, u32[]{:S(2)}, u32[]{:S(2)}) collective-permute-start(f32[2,8,512]{2,1,0:T(8,128)S(1)} %get-tuple-element.136.refs_0_), channel_id=1, source_target_pairs={{0,64},{32,96},{64,0},{96,32},{128,192},{160,224},{192,128},{224,1... | collective-permute-start | bytes 98312 | tf_op jit(solution)/shard_map/ppermute | solution.py:30
  58.6 2.7 %collective-permute-start.17 = (f32[16,512]{1,0:T(8,128)S(1)}, f32[16,512]{1,0:T(8,128)S(1)}, u32[]{:S(2)}, u32[]{:S(2)}) collective-permute-start(f32[16,512]{1,0:T(8,128)S(1)} %get-tuple-element.130.refs_0_), channel_id=1, source_target_pairs={{0,24},{1,25},{2,26},{3,27},{4,28},{5,29},{6,30},{7,31},{8,16},{9,... | collective-permute-start | bytes 98312 | tf_op jit(solution)/shard_map/ppermute | solution.py:30
  61.3 3.7 %collective-permute-start.19 = (f32[8,512]{1,0:T(8,128)S(1)}, f32[8,512]{1,0:T(8,128)S(1)}, u32[]{:S(2)}, u32[]{:S(2)}) collective-permute-start(f32[8,512]{1,0:T(8,128)S(1)} %get-tuple-element.141.refs_0_), channel_id=1, source_target_pairs={{0,192},{32,224},{64,128},{96,160},{128,64},{160,96},{192,0},{224,... | collective-permute-start | bytes 49160 | tf_op jit(solution)/shard_map/ppermute | solution.py:30
  65.0 1.6 %last_x.1 = (f32[128,512]{1,0:T(8,128)}, f32[128,512]{1,0:T(8,128)}, f32[8,128]{1,0:T(8,128)S(1)}) custom-call(f32[512,128]{1,0:T(8,128)S(1)} %get-tuple-element.134.refs_0_, f32[128,512]{1,0:T(8,128)S(1)} %get-tuple-element.79.refs_1_.refs_5_, f32[128,512]{1,0:T(8,128)S(1)} %get-tuple-element.78.refs_0_.refs_4_.refs_2_, ...), custom_call_target="tpu_custom_call" | custom-call | tf_op jit(solution)/shard_map/last_x/pallas_call | solution.py:500
  66.5 1.6 %end_z.1 = (f32[128,512]{1,0:T(8,128)}, f32[128,512]{1,0:T(8,128)}, f32[8,128]{1,0:T(8,128)S(1)}) custom-call(f32[16,512]{1,0:T(8,128)S(1)} %get-tuple-element.130.refs_0_, f32[16,512]{1,0:T(8,128)S(1)} %collective-permute-done.17.refs_1_, f32[16,512]{1,0:T(8,128)S(1)} %get-tuple-element.126.refs_3_.refs_2_, ...), custom_call_target="tpu_custom_call" | custom-call | tf_op jit(solution)/shard_map/end_z/pallas_call | solution.py:500
  (42 shorter events, 11.0 us)
Async XLA Ops:
  0.6 0.7 copy-start
  0.6 0.7 copy-start.1
  2.9 6.6 %collective-permute-start = (f32[16,512]{1,0:T(8,128)S(1)}, f32[16,512]{1,0:T(8,128)S(1)}, u32[]{:S(2)}, u32[]{:S(2)}) collective-permute-start(f32[16,512]{1,0:T(8,128)S(1)} %get-tuple-element.82), channel_id=1, source_target_pairs={{0,1},{2,3},{4,5},{6,7},{8,9},{10,11},{12,13},{14,15},{16,17},{18,... | collective-permute-start | bytes 98312 | tf_op jit(solution)/shard_map/ppermute | solution.py:25
  4.8 6.7 %collective-permute-start.1 = (f32[16,512]{1,0:T(8,128)S(1)}, f32[16,512]{1,0:T(8,128)S(1)}, u32[]{:S(2)}, u32[]{:S(2)}) collective-permute-start(f32[16,512]{1,0:T(8,128)S(1)} %get-tuple-element.83), channel_id=1, source_target_pairs={{1,2},{3,4},{5,6},{7,8},{9,10},{11,12},{13,14},{15,16},{17,18},{19... | collective-permute-start | bytes 98312 | tf_op jit(solution)/shard_map/ppermute | solution.py:25
  7.8 1.6 %collective-permute-start.2 = (f32[8,512]{1,0:T(8,128)S(1)}, f32[8,512]{1,0:T(8,128)S(1)}, u32[]{:S(2)}, u32[]{:S(2)}) collective-permute-start(f32[8,512]{1,0:T(8,128)S(1)} %get-tuple-element.90), channel_id=1, source_target_pairs={{0,32},{64,96},{128,160},{192,224},{32,0},{96,64},{160,128},{224,1... | collective-permute-start | bytes 49160 | tf_op jit(solution)/shard_map/ppermute | solution.py:25
  7.9 1.5 %collective-permute-start.3 = (f32[8,512]{1,0:T(8,128)S(1)}, f32[8,512]{1,0:T(8,128)S(1)}, u32[]{:S(2)}, u32[]{:S(2)}) collective-permute-start(f32[8,512]{1,0:T(8,128)S(1)} %get-tuple-element.91), channel_id=1, source_target_pairs={{32,64},{96,128},{160,192},{64,32},{128,96},{192,160},{33,65},{97,... | collective-permute-start | bytes 49160 | tf_op jit(solution)/shard_map/ppermute | solution.py:25
  12.4 5.4 %collective-permute-start.6 = (f32[5,16,512]{2,1,0:T(8,128)S(1)}, f32[5,16,512]{2,1,0:T(8,128)S(1)}, u32[]{:S(2)}, u32[]{:S(2)}) collective-permute-start(f32[5,16,512]{2,1,0:T(8,128)S(1)} %get-tuple-element.100.refs_0_), channel_id=1, source_target_pairs={{0,1},{1,0},{2,3},{3,2},{4,5},{5,4},{6,7},{7,6},{8,9},{9,8},{10,11... | collective-permute-start | bytes 491528 | tf_op jit(solution)/shard_map/ppermute | solution.py:30
  12.5 4.3 %collective-permute-start.4 = (f32[5,8,512]{2,1,0:T(8,128)S(1)}, f32[5,8,512]{2,1,0:T(8,128)S(1)}, u32[]{:S(2)}, u32[]{:S(2)}) collective-permute-start(f32[5,8,512]{2,1,0:T(8,128)S(1)} %get-tuple-element.93.refs_0_), channel_id=1, source_target_pairs={{0,32},{32,0},{64,96},{96,64},{128,160},{160,128},{192,224},{224,1... | collective-permute-start | bytes 245768 | tf_op jit(solution)/shard_map/ppermute | solution.py:30
  17.8 11.6 %collective-permute-start.8 = (f32[5,16,512]{2,1,0:T(8,128)S(1)}, f32[5,16,512]{2,1,0:T(8,128)S(1)}, u32[]{:S(2)}, u32[]{:S(2)}) collective-permute-start(f32[5,16,512]{2,1,0:T(8,128)S(1)} %get-tuple-element.109.refs_0_), channel_id=1, source_target_pairs={{0,2},{1,3},{2,0},{3,1},{4,6},{5,7},{6,4},{7,5},{8,10},{9,11},{10,... | collective-permute-start | bytes 491528 | tf_op jit(solution)/shard_map/ppermute | solution.py:30
  18.6 10.9 %collective-permute-start.5 = (f32[5,8,512]{2,1,0:T(8,128)S(1)}, f32[5,8,512]{2,1,0:T(8,128)S(1)}, u32[]{:S(2)}, u32[]{:S(2)}) collective-permute-start(f32[5,8,512]{2,1,0:T(8,128)S(1)} %get-tuple-element.99.refs_0_), channel_id=1, source_target_pairs={{0,64},{32,96},{64,0},{96,32},{128,192},{160,224},{192,128},{224,1... | collective-permute-start | bytes 245768 | tf_op jit(solution)/shard_map/ppermute | solution.py:30
  29.5 8.6 %collective-permute-start.10 = (f32[5,16,512]{2,1,0:T(8,128)S(1)}, f32[5,16,512]{2,1,0:T(8,128)S(1)}, u32[]{:S(2)}, u32[]{:S(2)}) collective-permute-start(f32[5,16,512]{2,1,0:T(8,128)S(1)} %get-tuple-element.112.refs_0_), channel_id=1, source_target_pairs={{0,6},{1,7},{2,4},{3,5},{4,2},{5,3},{6,0},{7,1},{8,14},{9,15},{10,... | collective-permute-start | bytes 491528 | tf_op jit(solution)/shard_map/ppermute | solution.py:30
  31.4 6.0 %collective-permute-start.7 = (f32[2,8,512]{2,1,0:T(8,128)S(1)}, f32[2,8,512]{2,1,0:T(8,128)S(1)}, u32[]{:S(2)}, u32[]{:S(2)}) collective-permute-start(f32[2,8,512]{2,1,0:T(8,128)S(1)} %get-tuple-element.104.refs_0_), channel_id=1, source_target_pairs={{0,192},{32,224},{64,128},{96,160},{128,64},{160,96},{192,0},{224,... | collective-permute-start | bytes 98312 | tf_op jit(solution)/shard_map/ppermute | solution.py:30
  38.2 6.9 %collective-permute-start.12 = (f32[5,16,512]{2,1,0:T(8,128)S(1)}, f32[5,16,512]{2,1,0:T(8,128)S(1)}, u32[]{:S(2)}, u32[]{:S(2)}) collective-permute-start(f32[5,16,512]{2,1,0:T(8,128)S(1)} %get-tuple-element.116.refs_0_), channel_id=1, source_target_pairs={{0,8},{1,9},{2,10},{3,11},{4,12},{5,13},{6,14},{7,15},{8,0},{9,1},... | collective-permute-start | bytes 491528 | tf_op jit(solution)/shard_map/ppermute | solution.py:30
  39.8 4.3 %collective-permute-start.9 = (f32[2,16,512]{2,1,0:T(8,128)S(1)}, f32[2,16,512]{2,1,0:T(8,128)S(1)}, u32[]{:S(2)}, u32[]{:S(2)}) collective-permute-start(f32[2,16,512]{2,1,0:T(8,128)S(1)} %get-tuple-element.111.refs_0_), channel_id=1, source_target_pairs={{0,1},{1,0},{2,3},{3,2},{4,5},{5,4},{6,7},{7,6},{8,9},{9,8},{10,11... | collective-permute-start | bytes 196616 | tf_op jit(solution)/shard_map/ppermute | solution.py:30
  44.1 4.4 %collective-permute-start.11 = (f32[2,16,512]{2,1,0:T(8,128)S(1)}, f32[2,16,512]{2,1,0:T(8,128)S(1)}, u32[]{:S(2)}, u32[]{:S(2)}) collective-permute-start(f32[2,16,512]{2,1,0:T(8,128)S(1)} %get-tuple-element.115.refs_0_), channel_id=1, source_target_pairs={{0,2},{1,3},{2,0},{3,1},{4,6},{5,7},{6,4},{7,5},{8,10},{9,11},{10,... | collective-permute-start | bytes 196616 | tf_op jit(solution)/shard_map/ppermute | solution.py:30
  45.2 5.6 %collective-permute-start.14 = (f32[2,16,512]{2,1,0:T(8,128)S(1)}, f32[2,16,512]{2,1,0:T(8,128)S(1)}, u32[]{:S(2)}, u32[]{:S(2)}) collective-permute-start(f32[2,16,512]{2,1,0:T(8,128)S(1)} %get-tuple-element.120.refs_0_), channel_id=1, source_target_pairs={{0,24},{1,25},{2,26},{3,27},{4,28},{5,29},{6,30},{7,31},{8,16},{9,... | collective-permute-start | bytes 196616 | tf_op jit(solution)/shard_map/ppermute | solution.py:30
  48.5 5.7 %collective-permute-start.13 = (f32[2,16,512]{2,1,0:T(8,128)S(1)}, f32[2,16,512]{2,1,0:T(8,128)S(1)}, u32[]{:S(2)}, u32[]{:S(2)}) collective-permute-start(f32[2,16,512]{2,1,0:T(8,128)S(1)} %get-tuple-element.119.refs_0_), channel_id=1, source_target_pairs={{0,6},{1,7},{2,4},{3,5},{4,2},{5,3},{6,0},{7,1},{8,14},{9,15},{10,... | collective-permute-start | bytes 196616 | tf_op jit(solution)/shard_map/ppermute | solution.py:30
  51.7 1.3 %collective-permute-start.15 = (f32[2,8,512]{2,1,0:T(8,128)S(1)}, f32[2,8,512]{2,1,0:T(8,128)S(1)}, u32[]{:S(2)}, u32[]{:S(2)}) collective-permute-start(f32[2,8,512]{2,1,0:T(8,128)S(1)} %get-tuple-element.125.refs_0_), channel_id=1, source_target_pairs={{0,32},{32,0},{64,96},{96,64},{128,160},{160,128},{192,224},{224,1... | collective-permute-start | bytes 98312 | tf_op jit(solution)/shard_map/ppermute | solution.py:30
  54.3 4.4 %collective-permute-start.16 = (f32[2,16,512]{2,1,0:T(8,128)S(1)}, f32[2,16,512]{2,1,0:T(8,128)S(1)}, u32[]{:S(2)}, u32[]{:S(2)}) collective-permute-start(f32[2,16,512]{2,1,0:T(8,128)S(1)} %get-tuple-element.128.refs_0_), channel_id=1, source_target_pairs={{0,8},{1,9},{2,10},{3,11},{4,12},{5,13},{6,14},{7,15},{8,0},{9,1},... | collective-permute-start | bytes 196616 | tf_op jit(solution)/shard_map/ppermute | solution.py:30
  54.8 6.5 %collective-permute-start.18 = (f32[2,8,512]{2,1,0:T(8,128)S(1)}, f32[2,8,512]{2,1,0:T(8,128)S(1)}, u32[]{:S(2)}, u32[]{:S(2)}) collective-permute-start(f32[2,8,512]{2,1,0:T(8,128)S(1)} %get-tuple-element.136.refs_0_), channel_id=1, source_target_pairs={{0,64},{32,96},{64,0},{96,32},{128,192},{160,224},{192,128},{224,1... | collective-permute-start | bytes 98312 | tf_op jit(solution)/shard_map/ppermute | solution.py:30
  58.6 7.9 %collective-permute-start.17 = (f32[16,512]{1,0:T(8,128)S(1)}, f32[16,512]{1,0:T(8,128)S(1)}, u32[]{:S(2)}, u32[]{:S(2)}) collective-permute-start(f32[16,512]{1,0:T(8,128)S(1)} %get-tuple-element.130.refs_0_), channel_id=1, source_target_pairs={{0,24},{1,25},{2,26},{3,27},{4,28},{5,29},{6,30},{7,31},{8,16},{9,... | collective-permute-start | bytes 98312 | tf_op jit(solution)/shard_map/ppermute | solution.py:30
  61.3 6.8 %collective-permute-start.19 = (f32[8,512]{1,0:T(8,128)S(1)}, f32[8,512]{1,0:T(8,128)S(1)}, u32[]{:S(2)}, u32[]{:S(2)}) collective-permute-start(f32[8,512]{1,0:T(8,128)S(1)} %get-tuple-element.141.refs_0_), channel_id=1, source_target_pairs={{0,192},{32,224},{64,128},{96,160},{128,64},{160,96},{192,0},{224,... | collective-permute-start | bytes 49160 | tf_op jit(solution)/shard_map/ppermute | solution.py:30

commit v3 on v2

--- a/solution.py
+++ b/solution.py
@@ -122,11 +122,9 @@
 
 
 def inputs_kernel(*refs):
-    away, (eps, mu), here = refs[:7], refs[7:9], refs[9:16]
-    y_even, y_odd, z_even, z_odd, tables, eps_s, mu_s, sems = refs[16:]
+    away, here = refs[:7], refs[7:14]
+    y_even, y_odd, z_even, z_odd, sems = refs[14:]
     copies = [pltpu.make_async_copy(away[i], here[i], sems.at[i]) for i in range(7)]
-    copies.append(pltpu.make_async_copy(eps, eps_s, sems.at[7]))
-    copies.append(pltpu.make_async_copy(mu, mu_s, sems.at[8]))
     for copy in copies:
         copy.start()
     for copy in copies:
@@ -162,9 +160,6 @@
 
     fill("gy", hx_last, ez_first, y_even, y_odd)
     fill("gz", hy_last, ex_first, z_even, z_odd)
-    for k in range(16):
-        tables[k:k + 1, :] = jnp.full((1, LANES), eps_s[k], F32)
-        tables[16 + k:17 + k, :] = jnp.full((1, LANES), mu_s[k], F32)
 
 
 def from_below(axis, even, odd):
@@ -175,8 +170,8 @@
     return jnp.where(jnp.broadcast_to(lax.axis_index(axis) & 1, even.shape) == 0, even, odd)
 
 
-def bands_kernel(material, tables, ie, ch, y_mat, z_mat, cy, cz):
-    spread = [jnp.broadcast_to(tables[k:k + 1, :], (NZL, LANES)) for k in range(32)]
+def bands_kernel(material, eps, mu, ie, ch, y_mat, z_mat, cy, cz):
+    spread = [jnp.full((NZL, LANES), table[k], F32) for table in (eps, mu) for k in range(16)]
     for y in range(NYL):
         for c in range(CHUNKS):
             label = material[plain(y), cut(c)]
@@ -521,22 +516,23 @@
     call = Order()
 
     inputs = (ex, ey, ez, hx, hy, hz, material)
-    ex, ey, ez, hx, hy, hz, material, y_even, y_odd, z_even, z_odd, tables = pl.pallas_call(
+    ex, ey, ez, hx, hy, hz, material, y_even, y_odd, z_even, z_odd = pl.pallas_call(
         inputs_kernel,
         out_shape=[jax.ShapeDtypeStruct(FIELD, a.dtype) for a in inputs]
-        + [shape(*Y1), shape(*Y1), shape(*Z1), shape(*Z1), shape(32, LANES)],
-        in_specs=[pl.BlockSpec(memory_space=pltpu.HBM)] * 9,
-        out_specs=[VM] * 12,
-        scratch_shapes=[pltpu.SMEM((16,), F32), pltpu.SMEM((16,), F32), pltpu.SemaphoreType.DMA((9,))],
+        + [shape(*Y1), shape(*Y1), shape(*Z1), shape(*Z1)],
+        in_specs=[pl.BlockSpec(memory_space=pltpu.HBM)] * 7,
+        out_specs=[VM] * 11,
+        scratch_shapes=[pltpu.SemaphoreType.DMA((7,))],
         compiler_params=pltpu.CompilerParams(vmem_limit_bytes=52 * 1024 * 1024),
         name="inputs",
-    )(*inputs, eps_table, mu_table)
+    )(*inputs)
     y_even, z_even = met(y_even, "gy", 0), met(z_even, "gz", 0)
     y_odd, z_odd = met(y_odd, "gy", 1), met(z_odd, "gz", 1)
 
     ie, ch, y_mat, z_mat, cy, cz = call(
-        bands_kernel, (material, tables),
-        (PACKED, PACKED, (3,) + Y1, (3,) + Z1, (45,) + Y1, (21,) + Z1), name="bands")
+        bands_kernel, (material, eps_table, mu_table),
+        (PACKED, PACKED, (3,) + Y1, (3,) + Z1, (45,) + Y1, (21,) + Z1),
+        specs=[VM] + [pl.BlockSpec(memory_space=pltpu.SMEM)] * 2, name="bands")
 
     pay_y, w_y, hz_t = call(first_y_kernel, (hz, ey, ex, hy, z_even, z_odd, ie, ch, y_mat, cy),
                             ((5,) + Y1, (15,) + Y1, PACKED), (PACKED, PACKED, Z1), after=(y_even, y_odd), name="first_y")

time: 69.3 us -> 68.5 us (0.988)
  transfers between devices with their start and end apart: 20 -> 20, of which waited for: 11 -> 11; matrix products, arithmetic and copies ran while one was open for 0% -> 0% of each run, Pallas kernels for 10% -> 11%
where the time goes in v3:
time: 68.5 us; the launch traced here: 68.4 us
  starting transfers between devices  41.2 us (60%)
  waiting for transfers between devices  15.1 us (22%)
  Pallas kernels  11.1 us (16%)
  between operations  0.9 us (1%)
    ppermute x16, starting transfers between devices, swapped(): return lax.ppermute(array, axis, [(i, i ^ flip) for i in range(size)])  35.5 us
    ppermute x16, waiting for transfers between devices, swapped(): return lax.ppermute(array, axis, [(i, i ^ flip) for i in range(size)])  13.6 us
    pallas_call x21, Pallas kernels, __call__(): pl.pallas_call(body, out_shape=[shape(*dims) for dims in outs], in_specs=...  9.59 us
    ppermute x4, starting transfers between devices, met(): lax.ppermute(array, axis, [(i, i + 1) for i in low] + [(i + 1, i) for i i...  5.69 us
    pallas_call x1, Pallas kernels, on_device(): pl.pallas_call(inputs_kernel, out_shape=[jax.ShapeDtypeStruct(FIELD, a.dt...  1.51 us
    ppermute x4, waiting for transfers between devices, met(): lax.ppermute(array, axis, [(i, i + 1) for i in low] + [(i + 1, i) for i i...  1.49 us
  transfers between devices with their start and end apart: 20, of which 11 were waited for; matrix products, arithmetic and copies ran while one was open for 0% of the time, Pallas kernels for 11%

profile of v3, /device:TPU:32, one launch (start us, length us, event | category | flops | bytes accessed | tf_op | source)
XLA Modules:
  0.0 68.4 jit_solution(4579754549883807446)
XLA Ops:
  0.6 1.5 %inputs.1 = (f32[128,512]{1,0:T(8,128)S(1)}, f32[128,512]{1,0:T(8,128)S(1)}, f32[128,512]{1,0:T(8,128)S(1)}, f32[128,512]{1,0:T(8,128)S(1)}, f32[128,512]{1,0:T(...) custom-call(f32[128,512]{1,0:T(8,128)} %bitcast.13, ...), custom_call_target="tpu_custom_call" | custom-call | tf_op jit(solution)/shard_map/inputs/pallas_call | solution.py:519
  2.2 1.9 %collective-permute-start = (f32[16,512]{1,0:T(8,128)S(1)}, f32[16,512]{1,0:T(8,128)S(1)}, u32[]{:S(2)}, u32[]{:S(2)}) collective-permute-start(f32[16,512]{1,0:T(8,128)S(1)} %get-tuple-element.81), channel_id=1, source_target_pairs={{0,1},{2,3},{4,5},{6,7},{8,9},{10,11},{12,13},{14,15},{16,17},{18,... | collective-permute-start | bytes 98312 | tf_op jit(solution)/shard_map/ppermute | solution.py:25
  4.1 3.0 %collective-permute-start.1 = (f32[16,512]{1,0:T(8,128)S(1)}, f32[16,512]{1,0:T(8,128)S(1)}, u32[]{:S(2)}, u32[]{:S(2)}) collective-permute-start(f32[16,512]{1,0:T(8,128)S(1)} %get-tuple-element.82), channel_id=1, source_target_pairs={{1,2},{3,4},{5,6},{7,8},{9,10},{11,12},{13,14},{15,16},{17,18},{19... | collective-permute-start | bytes 98312 | tf_op jit(solution)/shard_map/ppermute | solution.py:25
  7.9 1.3 %bands.1 = (f32[512,128]{1,0:T(8,128)S(1)}, f32[512,128]{1,0:T(8,128)S(1)}, f32[3,8,512]{2,1,0:T(8,128)S(1)}, f32[3,16,512]{2,1,0:T(8,128)S(1)}, f32[45,8,512]{2,1,0:T(8,128)S(1)}, /*index=5*/f32[21,16,512]{2,1,0:T(8,128)S(1)}) custom-call(s32[128,512]{1,0:T(8,128)S(1)} %get-tuple-element.83.refs_0_, f32[16]{0:T(128)S(1)} %copy-done, f32[16]{0:T(128)S(1)} %copy-done.1), custom_call_target="tpu_custom_call" | custom-call | tf_op jit(solution)/shard_map/bands/pallas_call | solution.py:495
  9.3 1.5 %collective-permute-done.1.refs_5_.refs_3_ = f32[16,512]{1,0:T(8,128)S(1)} collective-permute-done((f32[16,512]{1,0:T(8,128)S(1)}, f32[16,512]{1,0:T(8,128)S(1)}, u32[]{:S(2)}, u32[]{:S(2)}) %collective-permute-start.1) | collective-permute-done | bytes 32800 | tf_op jit(solution)/shard_map/ppermute | solution.py:25
  11.7 3.3 %collective-permute-start.4 = (f32[5,8,512]{2,1,0:T(8,128)S(1)}, f32[5,8,512]{2,1,0:T(8,128)S(1)}, u32[]{:S(2)}, u32[]{:S(2)}) collective-permute-start(f32[5,8,512]{2,1,0:T(8,128)S(1)} %get-tuple-element.91.refs_0_), channel_id=1, source_target_pairs={{0,32},{32,0},{64,96},{96,64},{128,160},{160,128},{192,224},{224,1... | collective-permute-start | bytes 245768 | tf_op jit(solution)/shard_map/ppermute | solution.py:30
  17.9 7.3 %collective-permute-start.5 = (f32[5,8,512]{2,1,0:T(8,128)S(1)}, f32[5,8,512]{2,1,0:T(8,128)S(1)}, u32[]{:S(2)}, u32[]{:S(2)}) collective-permute-start(f32[5,8,512]{2,1,0:T(8,128)S(1)} %get-tuple-element.97.refs_0_), channel_id=1, source_target_pairs={{0,64},{32,96},{64,0},{96,32},{128,192},{160,224},{192,128},{224,1... | collective-permute-start | bytes 245768 | tf_op jit(solution)/shard_map/ppermute | solution.py:30
  25.2 1.5 %first_x.1 = (f32[128,512]{1,0:T(8,128)S(1)}, f32[512,128]{1,0:T(8,128)S(1)}, f32[199,8,128]{2,1,0:T(8,128)S(1)}) custom-call(f32[128,512]{1,0:T(8,128)S(1)} %get-tuple-element.80.refs_3_.refs_0_.refs_8_, f32[128,512]{1,0:T(8,128)S(1)} %get-tuple-element.79.refs_2_.refs_1_.refs_10_, f32[16,512]{1,0:T(8,128)S(1)} %collective-permute-done.refs_4_.refs_2_, ...), custom_call_target="tpu_custom_call" | custom-call | tf_op jit(solution)/shard_map/first_x/pallas_call | solution.py:495
  26.7 2.0 %collective-permute-done.5.refs_1_ = f32[5,8,512]{2,1,0:T(8,128)S(1)} collective-permute-done((f32[5,8,512]{2,1,0:T(8,128)S(1)}, f32[5,8,512]{2,1,0:T(8,128)S(1)}, u32[]{:S(2)}, u32[]{:S(2)}) %collective-permute-start.5) | collective-permute-done | bytes 81952 | tf_op jit(solution)/shard_map/ppermute | solution.py:30
  28.8 1.9 %collective-permute-start.10 = (f32[5,16,512]{2,1,0:T(8,128)S(1)}, f32[5,16,512]{2,1,0:T(8,128)S(1)}, u32[]{:S(2)}, u32[]{:S(2)}) collective-permute-start(f32[5,16,512]{2,1,0:T(8,128)S(1)} %get-tuple-element.110.refs_0_), channel_id=1, source_target_pairs={{0,6},{1,7},{2,4},{3,5},{4,2},{5,3},{6,0},{7,1},{8,14},{9,15},{10,... | collective-permute-start | bytes 491528 | tf_op jit(solution)/shard_map/ppermute | solution.py:30
  30.7 4.0 %collective-permute-start.7 = (f32[2,8,512]{2,1,0:T(8,128)S(1)}, f32[2,8,512]{2,1,0:T(8,128)S(1)}, u32[]{:S(2)}, u32[]{:S(2)}) collective-permute-start(f32[2,8,512]{2,1,0:T(8,128)S(1)} %get-tuple-element.102.refs_0_), channel_id=1, source_target_pairs={{0,192},{32,224},{64,128},{96,160},{128,64},{160,96},{192,0},{224,... | collective-permute-start | bytes 98312 | tf_op jit(solution)/shard_map/ppermute | solution.py:30
  34.7 2.0 %collective-permute-done.7.refs_1_ = f32[2,8,512]{2,1,0:T(8,128)S(1)} collective-permute-done((f32[2,8,512]{2,1,0:T(8,128)S(1)}, f32[2,8,512]{2,1,0:T(8,128)S(1)}, u32[]{:S(2)}, u32[]{:S(2)}) %collective-permute-start.7) | collective-permute-done | bytes 32800 | tf_op jit(solution)/shard_map/ppermute | solution.py:30
  37.4 1.7 %collective-permute-start.12 = (f32[5,16,512]{2,1,0:T(8,128)S(1)}, f32[5,16,512]{2,1,0:T(8,128)S(1)}, u32[]{:S(2)}, u32[]{:S(2)}) collective-permute-start(f32[5,16,512]{2,1,0:T(8,128)S(1)} %get-tuple-element.114.refs_0_), channel_id=1, source_target_pairs={{0,8},{1,9},{2,10},{3,11},{4,12},{5,13},{6,14},{7,15},{8,0},{9,1},... | collective-permute-start | bytes 491528 | tf_op jit(solution)/shard_map/ppermute | solution.py:30
  39.1 1.3 %collective-permute-start.9 = (f32[2,16,512]{2,1,0:T(8,128)S(1)}, f32[2,16,512]{2,1,0:T(8,128)S(1)}, u32[]{:S(2)}, u32[]{:S(2)}) collective-permute-start(f32[2,16,512]{2,1,0:T(8,128)S(1)} %get-tuple-element.109.refs_0_), channel_id=1, source_target_pairs={{0,1},{1,0},{2,3},{3,2},{4,5},{5,4},{6,7},{7,6},{8,9},{9,8},{10,11... | collective-permute-start | bytes 196616 | tf_op jit(solution)/shard_map/ppermute | solution.py:30
  40.4 3.0 %collective-permute-done.9.refs_1_ = f32[2,16,512]{2,1,0:T(8,128)S(1)} collective-permute-done((f32[2,16,512]{2,1,0:T(8,128)S(1)}, f32[2,16,512]{2,1,0:T(8,128)S(1)}, u32[]{:S(2)}, u32[]{:S(2)}) %collective-permute-start.9) | collective-permute-done | bytes 65568 | tf_op jit(solution)/shard_map/ppermute | solution.py:30
  44.4 2.0 %collective-permute-start.14 = (f32[2,16,512]{2,1,0:T(8,128)S(1)}, f32[2,16,512]{2,1,0:T(8,128)S(1)}, u32[]{:S(2)}, u32[]{:S(2)}) collective-permute-start(f32[2,16,512]{2,1,0:T(8,128)S(1)} %get-tuple-element.118.refs_0_), channel_id=1, source_target_pairs={{0,24},{1,25},{2,26},{3,27},{4,28},{5,29},{6,30},{7,31},{8,16},{9,... | collective-permute-start | bytes 196616 | tf_op jit(solution)/shard_map/ppermute | solution.py:30
  46.4 1.3 %collective-permute-done.11.refs_1_ = f32[2,16,512]{2,1,0:T(8,128)S(1)} collective-permute-done((f32[2,16,512]{2,1,0:T(8,128)S(1)}, f32[2,16,512]{2,1,0:T(8,128)S(1)}, u32[]{:S(2)}, u32[]{:S(2)}) %collective-permute-start.11) | collective-permute-done | bytes 65568 | tf_op jit(solution)/shard_map/ppermute | solution.py:30
  47.7 1.8 %collective-permute-start.13 = (f32[2,16,512]{2,1,0:T(8,128)S(1)}, f32[2,16,512]{2,1,0:T(8,128)S(1)}, u32[]{:S(2)}, u32[]{:S(2)}) collective-permute-start(f32[2,16,512]{2,1,0:T(8,128)S(1)} %get-tuple-element.117.refs_0_), channel_id=1, source_target_pairs={{0,6},{1,7},{2,4},{3,5},{4,2},{5,3},{6,0},{7,1},{8,14},{9,15},{10,... | collective-permute-start | bytes 196616 | tf_op jit(solution)/shard_map/ppermute | solution.py:30
  52.2 1.3 %collective-permute-done.13.refs_1_ = f32[2,16,512]{2,1,0:T(8,128)S(1)} collective-permute-done((f32[2,16,512]{2,1,0:T(8,128)S(1)}, f32[2,16,512]{2,1,0:T(8,128)S(1)}, u32[]{:S(2)}, u32[]{:S(2)}) %collective-permute-start.13) | collective-permute-done | bytes 65568 | tf_op jit(solution)/shard_map/ppermute | solution.py:30
  54.1 3.4 %collective-permute-start.18 = (f32[2,8,512]{2,1,0:T(8,128)S(1)}, f32[2,8,512]{2,1,0:T(8,128)S(1)}, u32[]{:S(2)}, u32[]{:S(2)}) collective-permute-start(f32[2,8,512]{2,1,0:T(8,128)S(1)} %get-tuple-element.134.refs_0_), channel_id=1, source_target_pairs={{0,64},{32,96},{64,0},{96,32},{128,192},{160,224},{192,128},{224,1... | collective-permute-start | bytes 98312 | tf_op jit(solution)/shard_map/ppermute | solution.py:30
  57.9 2.6 %collective-permute-start.17 = (f32[16,512]{1,0:T(8,128)S(1)}, f32[16,512]{1,0:T(8,128)S(1)}, u32[]{:S(2)}, u32[]{:S(2)}) collective-permute-start(f32[16,512]{1,0:T(8,128)S(1)} %get-tuple-element.128.refs_0_), channel_id=1, source_target_pairs={{0,24},{1,25},{2,26},{3,27},{4,28},{5,29},{6,30},{7,31},{8,16},{9,... | collective-permute-start | bytes 98312 | tf_op jit(solution)/shard_map/ppermute | solution.py:30
  60.6 3.7 %collective-permute-start.19 = (f32[8,512]{1,0:T(8,128)S(1)}, f32[8,512]{1,0:T(8,128)S(1)}, u32[]{:S(2)}, u32[]{:S(2)}) collective-permute-start(f32[8,512]{1,0:T(8,128)S(1)} %get-tuple-element.139.refs_0_), channel_id=1, source_target_pairs={{0,192},{32,224},{64,128},{96,160},{128,64},{160,96},{192,0},{224,... | collective-permute-start | bytes 49160 | tf_op jit(solution)/shard_map/ppermute | solution.py:30
  64.3 1.5 %last_x.1 = (f32[128,512]{1,0:T(8,128)}, f32[128,512]{1,0:T(8,128)}, f32[8,128]{1,0:T(8,128)S(1)}) custom-call(f32[512,128]{1,0:T(8,128)S(1)} %get-tuple-element.132.refs_0_, f32[128,512]{1,0:T(8,128)S(1)} %get-tuple-element.78.refs_1_.refs_5_, f32[128,512]{1,0:T(8,128)S(1)} %get-tuple-element.77.refs_0_.refs_4_.refs_2_, ...), custom_call_target="tpu_custom_call" | custom-call | tf_op jit(solution)/shard_map/last_x/pallas_call | solution.py:495
  65.8 1.6 %end_z.1 = (f32[128,512]{1,0:T(8,128)}, f32[128,512]{1,0:T(8,128)}, f32[8,128]{1,0:T(8,128)S(1)}) custom-call(f32[16,512]{1,0:T(8,128)S(1)} %get-tuple-element.128.refs_0_, f32[16,512]{1,0:T(8,128)S(1)} %collective-permute-done.17.refs_1_, f32[16,512]{1,0:T(8,128)S(1)} %get-tuple-element.124.refs_3_.refs_2_, ...), custom_call_target="tpu_custom_call" | custom-call | tf_op jit(solution)/shard_map/end_z/pallas_call | solution.py:495
  (42 shorter events, 11.0 us)
Async XLA Ops:
  2.2 7.1 %collective-permute-start = (f32[16,512]{1,0:T(8,128)S(1)}, f32[16,512]{1,0:T(8,128)S(1)}, u32[]{:S(2)}, u32[]{:S(2)}) collective-permute-start(f32[16,512]{1,0:T(8,128)S(1)} %get-tuple-element.81), channel_id=1, source_target_pairs={{0,1},{2,3},{4,5},{6,7},{8,9},{10,11},{12,13},{14,15},{16,17},{18,... | collective-permute-start | bytes 98312 | tf_op jit(solution)/shard_map/ppermute | solution.py:25
  4.1 6.7 %collective-permute-start.1 = (f32[16,512]{1,0:T(8,128)S(1)}, f32[16,512]{1,0:T(8,128)S(1)}, u32[]{:S(2)}, u32[]{:S(2)}) collective-permute-start(f32[16,512]{1,0:T(8,128)S(1)} %get-tuple-element.82), channel_id=1, source_target_pairs={{1,2},{3,4},{5,6},{7,8},{9,10},{11,12},{13,14},{15,16},{17,18},{19... | collective-permute-start | bytes 98312 | tf_op jit(solution)/shard_map/ppermute | solution.py:25
  7.1 2.2 %collective-permute-start.2 = (f32[8,512]{1,0:T(8,128)S(1)}, f32[8,512]{1,0:T(8,128)S(1)}, u32[]{:S(2)}, u32[]{:S(2)}) collective-permute-start(f32[8,512]{1,0:T(8,128)S(1)} %get-tuple-element.88), channel_id=1, source_target_pairs={{0,32},{64,96},{128,160},{192,224},{32,0},{96,64},{160,128},{224,1... | collective-permute-start | bytes 49160 | tf_op jit(solution)/shard_map/ppermute | solution.py:25
  7.2 0.7 %copy-start = (f32[16]{0:T(128)S(1)}, f32[16]{0:T(128)}, u32[]{:S(2)}) copy-start(f32[16]{0:T(128)} %refs_1_.1) | copy-start | bytes 196
  7.2 0.7 %copy-start.1 = (f32[16]{0:T(128)S(1)}, f32[16]{0:T(128)}, u32[]{:S(2)}) copy-start(f32[16]{0:T(128)} %refs_2_.1) | copy-start | bytes 196
  7.2 2.1 %collective-permute-start.3 = (f32[8,512]{1,0:T(8,128)S(1)}, f32[8,512]{1,0:T(8,128)S(1)}, u32[]{:S(2)}, u32[]{:S(2)}) collective-permute-start(f32[8,512]{1,0:T(8,128)S(1)} %get-tuple-element.89), channel_id=1, source_target_pairs={{32,64},{96,128},{160,192},{64,32},{128,96},{192,160},{33,65},{97,... | collective-permute-start | bytes 49160 | tf_op jit(solution)/shard_map/ppermute | solution.py:25
  11.6 5.4 %collective-permute-start.6 = (f32[5,16,512]{2,1,0:T(8,128)S(1)}, f32[5,16,512]{2,1,0:T(8,128)S(1)}, u32[]{:S(2)}, u32[]{:S(2)}) collective-permute-start(f32[5,16,512]{2,1,0:T(8,128)S(1)} %get-tuple-element.98.refs_0_), channel_id=1, source_target_pairs={{0,1},{1,0},{2,3},{3,2},{4,5},{5,4},{6,7},{7,6},{8,9},{9,8},{10,11... | collective-permute-start | bytes 491528 | tf_op jit(solution)/shard_map/ppermute | solution.py:30
  11.7 4.2 %collective-permute-start.4 = (f32[5,8,512]{2,1,0:T(8,128)S(1)}, f32[5,8,512]{2,1,0:T(8,128)S(1)}, u32[]{:S(2)}, u32[]{:S(2)}) collective-permute-start(f32[5,8,512]{2,1,0:T(8,128)S(1)} %get-tuple-element.91.refs_0_), channel_id=1, source_target_pairs={{0,32},{32,0},{64,96},{96,64},{128,160},{160,128},{192,224},{224,1... | collective-permute-start | bytes 245768 | tf_op jit(solution)/shard_map/ppermute | solution.py:30
  17.0 11.7 %collective-permute-start.8 = (f32[5,16,512]{2,1,0:T(8,128)S(1)}, f32[5,16,512]{2,1,0:T(8,128)S(1)}, u32[]{:S(2)}, u32[]{:S(2)}) collective-permute-start(f32[5,16,512]{2,1,0:T(8,128)S(1)} %get-tuple-element.107.refs_0_), channel_id=1, source_target_pairs={{0,2},{1,3},{2,0},{3,1},{4,6},{5,7},{6,4},{7,5},{8,10},{9,11},{10,... | collective-permute-start | bytes 491528 | tf_op jit(solution)/shard_map/ppermute | solution.py:30
  17.9 10.8 %collective-permute-start.5 = (f32[5,8,512]{2,1,0:T(8,128)S(1)}, f32[5,8,512]{2,1,0:T(8,128)S(1)}, u32[]{:S(2)}, u32[]{:S(2)}) collective-permute-start(f32[5,8,512]{2,1,0:T(8,128)S(1)} %get-tuple-element.97.refs_0_), channel_id=1, source_target_pairs={{0,64},{32,96},{64,0},{96,32},{128,192},{160,224},{192,128},{224,1... | collective-permute-start | bytes 245768 | tf_op jit(solution)/shard_map/ppermute | solution.py:30
  28.8 8.6 %collective-permute-start.10 = (f32[5,16,512]{2,1,0:T(8,128)S(1)}, f32[5,16,512]{2,1,0:T(8,128)S(1)}, u32[]{:S(2)}, u32[]{:S(2)}) collective-permute-start(f32[5,16,512]{2,1,0:T(8,128)S(1)} %get-tuple-element.110.refs_0_), channel_id=1, source_target_pairs={{0,6},{1,7},{2,4},{3,5},{4,2},{5,3},{6,0},{7,1},{8,14},{9,15},{10,... | collective-permute-start | bytes 491528 | tf_op jit(solution)/shard_map/ppermute | solution.py:30
  30.7 6.0 %collective-permute-start.7 = (f32[2,8,512]{2,1,0:T(8,128)S(1)}, f32[2,8,512]{2,1,0:T(8,128)S(1)}, u32[]{:S(2)}, u32[]{:S(2)}) collective-permute-start(f32[2,8,512]{2,1,0:T(8,128)S(1)} %get-tuple-element.102.refs_0_), channel_id=1, source_target_pairs={{0,192},{32,224},{64,128},{96,160},{128,64},{160,96},{192,0},{224,... | collective-permute-start | bytes 98312 | tf_op jit(solution)/shard_map/ppermute | solution.py:30
  37.4 6.9 %collective-permute-start.12 = (f32[5,16,512]{2,1,0:T(8,128)S(1)}, f32[5,16,512]{2,1,0:T(8,128)S(1)}, u32[]{:S(2)}, u32[]{:S(2)}) collective-permute-start(f32[5,16,512]{2,1,0:T(8,128)S(1)} %get-tuple-element.114.refs_0_), channel_id=1, source_target_pairs={{0,8},{1,9},{2,10},{3,11},{4,12},{5,13},{6,14},{7,15},{8,0},{9,1},... | collective-permute-start | bytes 491528 | tf_op jit(solution)/shard_map/ppermute | solution.py:30
  39.1 4.3 %collective-permute-start.9 = (f32[2,16,512]{2,1,0:T(8,128)S(1)}, f32[2,16,512]{2,1,0:T(8,128)S(1)}, u32[]{:S(2)}, u32[]{:S(2)}) collective-permute-start(f32[2,16,512]{2,1,0:T(8,128)S(1)} %get-tuple-element.109.refs_0_), channel_id=1, source_target_pairs={{0,1},{1,0},{2,3},{3,2},{4,5},{5,4},{6,7},{7,6},{8,9},{9,8},{10,11... | collective-permute-start | bytes 196616 | tf_op jit(solution)/shard_map/ppermute | solution.py:30
  43.4 4.4 %collective-permute-start.11 = (f32[2,16,512]{2,1,0:T(8,128)S(1)}, f32[2,16,512]{2,1,0:T(8,128)S(1)}, u32[]{:S(2)}, u32[]{:S(2)}) collective-permute-start(f32[2,16,512]{2,1,0:T(8,128)S(1)} %get-tuple-element.113.refs_0_), channel_id=1, source_target_pairs={{0,2},{1,3},{2,0},{3,1},{4,6},{5,7},{6,4},{7,5},{8,10},{9,11},{10,... | collective-permute-start | bytes 196616 | tf_op jit(solution)/shard_map/ppermute | solution.py:30
  44.4 5.6 %collective-permute-start.14 = (f32[2,16,512]{2,1,0:T(8,128)S(1)}, f32[2,16,512]{2,1,0:T(8,128)S(1)}, u32[]{:S(2)}, u32[]{:S(2)}) collective-permute-start(f32[2,16,512]{2,1,0:T(8,128)S(1)} %get-tuple-element.118.refs_0_), channel_id=1, source_target_pairs={{0,24},{1,25},{2,26},{3,27},{4,28},{5,29},{6,30},{7,31},{8,16},{9,... | collective-permute-start | bytes 196616 | tf_op jit(solution)/shard_map/ppermute | solution.py:30
  47.7 5.7 %collective-permute-start.13 = (f32[2,16,512]{2,1,0:T(8,128)S(1)}, f32[2,16,512]{2,1,0:T(8,128)S(1)}, u32[]{:S(2)}, u32[]{:S(2)}) collective-permute-start(f32[2,16,512]{2,1,0:T(8,128)S(1)} %get-tuple-element.117.refs_0_), channel_id=1, source_target_pairs={{0,6},{1,7},{2,4},{3,5},{4,2},{5,3},{6,0},{7,1},{8,14},{9,15},{10,... | collective-permute-start | bytes 196616 | tf_op jit(solution)/shard_map/ppermute | solution.py:30
  50.9 1.3 %collective-permute-start.15 = (f32[2,8,512]{2,1,0:T(8,128)S(1)}, f32[2,8,512]{2,1,0:T(8,128)S(1)}, u32[]{:S(2)}, u32[]{:S(2)}) collective-permute-start(f32[2,8,512]{2,1,0:T(8,128)S(1)} %get-tuple-element.123.refs_0_), channel_id=1, source_target_pairs={{0,32},{32,0},{64,96},{96,64},{128,160},{160,128},{192,224},{224,1... | collective-permute-start | bytes 98312 | tf_op jit(solution)/shard_map/ppermute | solution.py:30
  53.5 4.4 %collective-permute-start.16 = (f32[2,16,512]{2,1,0:T(8,128)S(1)}, f32[2,16,512]{2,1,0:T(8,128)S(1)}, u32[]{:S(2)}, u32[]{:S(2)}) collective-permute-start(f32[2,16,512]{2,1,0:T(8,128)S(1)} %get-tuple-element.126.refs_0_), channel_id=1, source_target_pairs={{0,8},{1,9},{2,10},{3,11},{4,12},{5,13},{6,14},{7,15},{8,0},{9,1},... | collective-permute-start | bytes 196616 | tf_op jit(solution)/shard_map/ppermute | solution.py:30
  54.1 6.5 %collective-permute-start.18 = (f32[2,8,512]{2,1,0:T(8,128)S(1)}, f32[2,8,512]{2,1,0:T(8,128)S(1)}, u32[]{:S(2)}, u32[]{:S(2)}) collective-permute-start(f32[2,8,512]{2,1,0:T(8,128)S(1)} %get-tuple-element.134.refs_0_), channel_id=1, source_target_pairs={{0,64},{32,96},{64,0},{96,32},{128,192},{160,224},{192,128},{224,1... | collective-permute-start | bytes 98312 | tf_op jit(solution)/shard_map/ppermute | solution.py:30
  57.9 7.9 %collective-permute-start.17 = (f32[16,512]{1,0:T(8,128)S(1)}, f32[16,512]{1,0:T(8,128)S(1)}, u32[]{:S(2)}, u32[]{:S(2)}) collective-permute-start(f32[16,512]{1,0:T(8,128)S(1)} %get-tuple-element.128.refs_0_), channel_id=1, source_target_pairs={{0,24},{1,25},{2,26},{3,27},{4,28},{5,29},{6,30},{7,31},{8,16},{9,... | collective-permute-start | bytes 98312 | tf_op jit(solution)/shard_map/ppermute | solution.py:30
  60.6 6.9 %collective-permute-start.19 = (f32[8,512]{1,0:T(8,128)S(1)}, f32[8,512]{1,0:T(8,128)S(1)}, u32[]{:S(2)}, u32[]{:S(2)}) collective-permute-start(f32[8,512]{1,0:T(8,128)S(1)} %get-tuple-element.139.refs_0_), channel_id=1, source_target_pairs={{0,192},{32,224},{64,128},{96,160},{128,64},{160,96},{192,0},{224,... | collective-permute-start | bytes 49160 | tf_op jit(solution)/shard_map/ppermute | solution.py:30
